TPU v7x, 512 devices: a whole 4x8x8 slice. The times are simulated.
512 devices in a mesh: prompt: 4 (over y_hi), sample: 16 (over y_lo, x, core), tensor: 8 (over z).
Axes of the slice: x: 4, y: 8 (y_hi: 4, y_lo: 2; y = y_hi * 2 + y_lo), z: 8, core: 2. Of those that a mesh axis runs over, the one named last changes fastest.
Arguments:
- hidden_in: float32 [1536, 5120], P('prompt', 'sample'), parts along dimension 0, may hold values from -12 to 12
- prompt_len: int32 [16], P('prompt'), parts along dimension 0, may hold values from 1 to 1024, 2048 in all
- cached_prompt_keys: bfloat16 [2, 8192, 8, 128], P(None, ('prompt', 'sample'), 'tensor'), parts along dimension 1, may hold values from -900 to 900
- cached_prompt_values: bfloat16 [2, 8192, 8, 128], P(None, ('prompt', 'sample'), 'tensor'), parts along dimension 1, may hold values from -6 to 6
- query_key_value_weight: bfloat16 [2, 5120, 10240], P(None, 'sample', 'tensor'), may hold values from -1 to 1
- w_out: bfloat16 [2, 8192, 5120], P(None, 'tensor', 'sample'), may hold values from -0.0625 to 0.0625
Outputs:
- hidden_out: float32 [1536, 5120], P('prompt', 'sample'), parts along dimension 0
There are 4 independent parts, one for each index of `prompt`. A program takes and returns all parts, laid end to end along the dimension named above; an argument that names none is the same for every part. Nothing has to cross between parts.
Inputs may be any that keep to these rules, and one draw needn't show every extreme that they name: `prompt_len`: the lengths sum to 2048, and one of them is exactly 1024.
All inputs are finite; a program needn't handle non-finite values.
Results may differ from a plain program's by a relative error of at most 0.0065.
Values may be sent and summed in bfloat16 or wider, within the bound.
A program may use at most 64 MiB of HBM per device.

v0:
```python
import jax
import jax.numpy as jnp
from jax import lax
from jax.sharding import PartitionSpec as P

QUERY_HEADS = 64
KEY_VALUE_HEADS = 8
LAYER_TOTAL = 2
STEPS = 6
NPR = 4


rope_base = 1000000.0
epsilon = 1e-06
score_after_mask = -1e30


def rotate(vector, positions):
    half_dim = vector.shape[-1] // 2
    frequency = rope_base ** (-2.0 * jnp.arange(half_dim, dtype=jnp.float32) / vector.shape[-1])
    target_shape = (positions.shape[0],) + (1,) * (vector.ndim - 2) + (half_dim,)
    angles = (positions[:, None] * frequency[None, :]).reshape(target_shape)
    cosine = jnp.cos(angles)
    sine_part = jnp.sin(angles)
    leading = vector[..., :half_dim]
    trailing = vector[..., half_dim:]
    return jnp.concatenate(
        [leading * cosine - trailing * sine_part, trailing * cosine + leading * sine_part], axis=-1
    )


def softmax_parts(scores, visible):
    scores = jnp.where(visible, scores, score_after_mask)
    maxima = jnp.max(scores, axis=-1)
    weights = jnp.where(visible, jnp.exp(scores - maxima[..., None]), 0.0)
    totals = jnp.sum(weights, axis=-1)
    return (maxima, weights.astype(jnp.bfloat16), totals)


def block_stats(queries, keys, values, visible):
    scale_factor = keys.shape[-1] ** (-0.5)
    scores = (
        jnp.einsum(
            "rgqd,ngd->rgqn",
            queries,
            keys.astype(jnp.float32),
            precision=lax.Precision.HIGHEST,
            preferred_element_type=jnp.float32,
        )
        * scale_factor
    )
    maxima, rounded, totals = softmax_parts(scores, visible[:, None, None, :])
    partial_value = jnp.einsum(
        "rgqn,ngd->rgqd", rounded, values, preferred_element_type=jnp.float32
    )
    return (maxima, partial_value, totals)


def recent_stats(queries, new_keys, new_values):
    number_of_rows, kv_heads, queries_per_group, head_dim = queries.shape
    samples_here = number_of_rows // STEPS
    query_view = queries.reshape(samples_here, STEPS, kv_heads, queries_per_group, head_dim)
    key_view = new_keys.reshape(samples_here, STEPS, kv_heads, head_dim).astype(jnp.float32)
    value_view = new_values.reshape(samples_here, STEPS, kv_heads, head_dim)
    scores = jnp.einsum(
        "stgqd,sugd->stgqu",
        query_view,
        key_view,
        precision=lax.Precision.HIGHEST,
        preferred_element_type=jnp.float32,
    ) * head_dim ** (-0.5)
    steps_here = jnp.arange(STEPS, dtype=jnp.int32)
    visible = (steps_here[None, :] <= steps_here[:, None])[None, :, None, None, :]
    maxima, rounded, totals = softmax_parts(scores, visible)
    partial_value = jnp.einsum(
        "stgqu,sugd->stgqd", rounded, value_view, preferred_element_type=jnp.float32
    )
    return (
        maxima.reshape(number_of_rows, kv_heads, queries_per_group),
        partial_value.reshape(number_of_rows, kv_heads, queries_per_group, head_dim),
        totals.reshape(number_of_rows, kv_heads, queries_per_group),
    )


def combine(earlier, later):
    peak = jnp.maximum(earlier[0], later[0])
    scale_left = jnp.exp(earlier[0] - peak)
    scale_right = jnp.exp(later[0] - peak)
    return (
        peak,
        earlier[1] * scale_left[..., None] + later[1] * scale_right[..., None],
        earlier[2] * scale_left + later[2] * scale_right,
    )


def on_device(
    hidden_in, prompt_len, cached_prompt_keys, cached_prompt_values, query_key_value_weight, w_out
):
    sample_count = lax.axis_size("sample")
    device_index = lax.axis_index("sample")
    number_of_rows = hidden_in.shape[0]
    rows_dev = number_of_rows // sample_count
    kv_dev = cached_prompt_keys.shape[2]
    head_dim = cached_prompt_keys.shape[3]
    key_block = cached_prompt_keys.shape[1]
    queries_per_group = QUERY_HEADS // KEY_VALUE_HEADS
    width = hidden_in.shape[1] * sample_count
    row_ids = jnp.arange(number_of_rows, dtype=jnp.int32)
    prompt_of = row_ids // STEPS % NPR
    onehot = prompt_of[:, None] == jnp.arange(NPR, dtype=jnp.int32)[None, :]
    offsets = jnp.cumsum(prompt_len) - prompt_len
    row_len = jnp.sum(jnp.where(onehot, prompt_len[None, :], 0), axis=1)
    row_start = jnp.sum(jnp.where(onehot, offsets[None, :], 0), axis=1)
    row_end = row_start + row_len
    positions = (row_len + row_ids % STEPS).astype(jnp.float32)
    own_first = device_index * rows_dev
    own_positions = lax.dynamic_slice_in_dim(positions, own_first, rows_dev, 0)
    own_start = lax.dynamic_slice_in_dim(row_start, own_first, rows_dev, 0)
    own_end = lax.dynamic_slice_in_dim(row_end, own_first, rows_dev, 0)
    stream = hidden_in
    for layer_position in range(LAYER_TOTAL):
        total_squares = lax.psum(jnp.sum(stream * stream, axis=1), "sample")
        inverse_root_mean = lax.rsqrt(total_squares / width + epsilon)
        stream_half = stream.astype(jnp.bfloat16)
        weights_in = query_key_value_weight[layer_position]

        def project(first_row, row_total, weights_in=weights_in, stream_half=stream_half):
            return jnp.dot(stream_half, weights_in, preferred_element_type=jnp.float32)

        weighted_values = lax.psum_scatter(
            project(jnp.int32(0), rows_dev * lax.axis_size("sample")),
            "sample",
            scatter_dimension=0,
            tiled=True,
        )
        own_inv = lax.dynamic_slice_in_dim(inverse_root_mean, own_first, rows_dev, 0)
        weighted_values = (weighted_values * own_inv[:, None]).reshape(
            rows_dev, kv_dev, queries_per_group + 2, head_dim
        )
        queries = rotate(weighted_values[:, :, :queries_per_group, :], own_positions)
        new_keys = rotate(weighted_values[:, :, queries_per_group, :], own_positions).astype(
            jnp.bfloat16
        )
        new_values = weighted_values[:, :, queries_per_group + 1, :].astype(jnp.bfloat16)
        keys_here = cached_prompt_keys[layer_position]
        values_here = cached_prompt_values[layer_position]

        def fold_prompt(running, pieces, first_row, queries=queries):
            keys_piece, values_piece = pieces
            block_count = keys_piece.shape[0] // key_block
            keys_split = keys_piece.reshape(block_count, key_block, kv_dev, head_dim)
            values_split = values_piece.reshape(block_count, key_block, kv_dev, head_dim)

            def visit(inner, items):
                keys_blk, values_blk, block_number = items
                key_pos = block_number * key_block + jnp.arange(key_block, dtype=jnp.int32)
                visible = (key_pos[None, :] >= own_start[:, None]) & (
                    key_pos[None, :] < own_end[:, None]
                )
                return (combine(inner, block_stats(queries, keys_blk, values_blk, visible)), None)

            running, ignored = lax.scan(
                visit, running, (keys_split, values_split, jnp.arange(block_count, dtype=jnp.int32))
            )
            return running

        starting_value = (
            jnp.full((rows_dev, kv_dev, queries_per_group), score_after_mask, jnp.float32),
            jnp.zeros((rows_dev, kv_dev, queries_per_group, head_dim), jnp.float32),
            jnp.zeros((rows_dev, kv_dev, queries_per_group), jnp.float32),
        )
        summary = fold_prompt(
            starting_value,
            (
                lax.all_gather(keys_here, "sample", axis=0, tiled=True),
                lax.all_gather(values_here, "sample", axis=0, tiled=True),
            ),
            jnp.int32(0),
        )
        summary = combine(summary, recent_stats(queries, new_keys, new_values))
        attention = (
            (summary[1] / summary[2][..., None])
            .astype(jnp.bfloat16)
            .reshape(rows_dev, kv_dev * queries_per_group * head_dim)
        )
        out_weights = w_out[layer_position]

        def apply_out(segment, first_row, out_weights=out_weights):
            return jnp.dot(segment, out_weights, preferred_element_type=jnp.float32)

        partial_out = apply_out(
            lax.all_gather(attention, "sample", axis=0, tiled=True), jnp.int32(0)
        )
        update = lax.psum(partial_out, "tensor")
        stream = stream + update
    return stream


def solution(mesh):
    return jax.shard_map(
        on_device,
        mesh=mesh,
        in_specs=(
            P("prompt", "sample"),
            P("prompt"),
            P(None, ("prompt", "sample"), "tensor", None),
            P(None, ("prompt", "sample"), "tensor", None),
            P(None, "sample", "tensor"),
            P(None, "tensor", "sample"),
        ),
        out_specs=P("prompt", "sample"),
        check_vma=False,
    )
```

profile of v0, /device:TPU:1, one launch (start us, length us, event | category | flops | bytes accessed | tf_op | source)
XLA Modules:
  0.0 436.7 jit_solution(14882734858727554392)
XLA Ops:
  6.5 3.3 fusion.54
  11.0 33.4 %psum.28 = f32[384]{0:T(512)S(1)} all-reduce(f32[384]{0:T(512)S(1)} %multiply_reduce_fusion.1), channel_id=1, replica_groups=mesh['prompt'=4,'sample'=16,'tensor'=8] {'sample'}, use_global_device_ids=true, to_apply=%region_5.6 | all-reduce | flops 384 | bytes 3072 | tf_op jit(solution)/shard_map/psum | solution.py:122
  44.7 18.1 %all-gather = bf16[1,2048,1,128]{3,1,2,0:T(8,128)(2,1)S(1)} all-gather(bf16[1,128,1,128]{3,1,2,0:T(8,128)(2,1)S(1)} %get-tuple-element.308), channel_id=2, replica_groups=mesh['prompt'=4,'sample'=16,'tensor'=8] {'sample'}, dimensions={1}, use_global_device_ids=true | all-gather | bytes 557056 | tf_op jit(solution)/shard_map/all_gather | solution.py:175
  62.9 19.9 %all-gather.1 = bf16[1,2048,1,128]{3,1,2,0:T(8,128)(2,1)S(1)} all-gather(bf16[1,128,1,128]{3,1,2,0:T(8,128)(2,1)S(1)} %get-tuple-element.306), channel_id=3, replica_groups=mesh['prompt'=4,'sample'=16,'tensor'=8] {'sample'}, dimensions={1}, use_global_device_ids=true | all-gather | bytes 557056 | tf_op jit(solution)/shard_map/all_gather | solution.py:176
  82.8 1.0 broadcast_multiply_fusion.1
  84.3 0.8 fusion.139
  85.3 35.8 %while.30 = (s32[]{:T(128)}, f32[24,1,8]{0,2,1:T(8,128)S(1)}, f32[24,1,8,128]{3,0,2,1:T(8,128)S(1)}, f32[24,1,8]{0,2,1:T(8,128)S(1)}, s32[16]{0:T(128)S(1)}, /*i...) while((s32[]{:T(128)}, f32[24,1,8]{0,2,1:T(8,128)S(1)}, ...), condition=%wide.region_9.10_spmd.clone, body=%wide.region_6.9_spmd.clone.sunk | while | flops 44370752 | bytes 693613 | solution.py:162
  85.3 0.7 dynamic_slice.74
  87.6 0.7 dynamic_slice.74
  94.3 0.7 dynamic_slice.74
  96.5 0.7 dynamic_slice.74
  98.8 0.7 dynamic_slice.74
  101.0 0.7 dynamic_slice.74
  103.2 0.7 dynamic_slice.74
  105.5 0.7 dynamic_slice.74
  107.7 0.7 dynamic_slice.74
  121.6 20.8 %all_gather.20 = bf16[384,1024]{1,0:T(8,128)(2,1)S(1)} all-gather(bf16[24,1024]{1,0:T(8,128)(2,1)S(1)} %bitcast.267), channel_id=1, replica_groups=mesh['prompt'=4,'sample'=16,'tensor'=8] {'sample'}, dimensions={0}, use_global_device_ids=true | all-gather | bytes 835584 | tf_op jit(solution)/shard_map/all_gather | solution.py:192
  142.4 2.5 fusion.60
  145.0 74.5 %all-reduce.3.cloned.1.call-done = f32[384,320]{0,1:T(8,128)} async-done(((f32[384,320]{0,1:T(8,128)}), f32[384,320]{0,1:T(8,128)}) %all-reduce.3.cloned.1.call-update) | async-done | bytes 491536 | tf_op jit(solution)/shard_map/psum | solution.py:194
  219.5 1.1 multiply_reduce_fusion
  220.6 2.0 fusion.52
  222.7 26.3 %all-gather.2 = bf16[1,2048,1,128]{3,1,2,0:T(8,128)(2,1)S(1)} all-gather(bf16[1,128,1,128]{3,1,2,0:T(8,128)(2,1)S(1)} %get-tuple-element.307), channel_id=4, replica_groups=mesh['prompt'=4,'sample'=16,'tensor'=8] {'sample'}, dimensions={1}, use_global_device_ids=true | all-gather | bytes 557056 | tf_op jit(solution)/shard_map/all_gather | solution.py:175
  249.0 18.2 %all-gather.3 = bf16[1,2048,1,128]{3,1,2,0:T(8,128)(2,1)S(1)} all-gather(bf16[1,128,1,128]{3,1,2,0:T(8,128)(2,1)S(1)} %get-tuple-element.305), channel_id=5, replica_groups=mesh['prompt'=4,'sample'=16,'tensor'=8] {'sample'}, dimensions={1}, use_global_device_ids=true | all-gather | bytes 557056 | tf_op jit(solution)/shard_map/all_gather | solution.py:176
  267.2 26.7 %psum.30 = f32[384]{0:T(512)S(1)} all-reduce(f32[384]{0:T(512)S(1)} %get-tuple-element.291), channel_id=1, replica_groups=mesh['prompt'=4,'sample'=16,'tensor'=8] {'sample'}, use_global_device_ids=true, to_apply=%region_15.16 | all-reduce | flops 384 | bytes 3072 | tf_op jit(solution)/shard_map/psum | solution.py:122
  294.0 1.0 broadcast_multiply_fusion
  295.5 0.8 fusion.140
  296.5 35.8 %while.31 = (s32[]{:T(128)}, f32[24,1,8]{0,2,1:T(8,128)S(1)}, f32[24,1,8,128]{3,0,2,1:T(8,128)S(1)}, f32[24,1,8]{0,2,1:T(8,128)S(1)}, s32[16]{0:T(128)S(1)}, /*i...) while((s32[]{:T(128)}, f32[24,1,8]{0,2,1:T(8,128)S(1)}, ...), condition=%wide.region_19.20_spmd.clone, body=%wide.region_16.19_spmd.clone.sunk | while | flops 44370752 | bytes 693613 | solution.py:162
  296.5 0.7 dynamic_slice.77
  332.8 20.2 %all_gather.23 = bf16[384,1024]{1,0:T(8,128)(2,1)S(1)} all-gather(bf16[24,1024]{1,0:T(8,128)(2,1)S(1)} %bitcast.268), channel_id=1, replica_groups=mesh['prompt'=4,'sample'=16,'tensor'=8] {'sample'}, dimensions={0}, use_global_device_ids=true | all-gather | bytes 835584 | tf_op jit(solution)/shard_map/all_gather | solution.py:192
  353.0 2.4 fusion.58
  355.4 72.9 %all-reduce.5.cloned.1.call-done = f32[384,320]{0,1:T(8,128)} async-done(((f32[384,320]{0,1:T(8,128)}), f32[384,320]{0,1:T(8,128)}) %all-reduce.5.cloned.1.call-update) | async-done | bytes 491536 | tf_op jit(solution)/shard_map/psum | solution.py:194
  428.3 1.9 add.136
  (364 shorter events, 44.5 us)
Async XLA Ops:
  6.5 76.3 %reduce-scatter.3.cloned.1.call-start = ((), (), s32[]{:S(2)}) async-start(), calls=%async_computation.2 | async-start | bytes 2088960 | tf_op jit(solution)/shard_map/reduce_scatter | solution.py:130
  9.8 0.7 copy-start.4
  9.8 1.1 copy-start
  9.8 34.9 %copy-start.2 = (bf16[2,128,1,128]{3,1,2,0:T(8,128)(2,1)S(1)}, bf16[2,128,1,128]{3,1,2,0:T(8,128)(2,1)}, u32[]{:S(2)}) copy-start(bf16[2,128,1,128]{3,1,2,0:T(8,128)(2,1)} %param.12) | copy-start | bytes 196612
  9.8 34.9 %copy-start.3 = (bf16[2,128,1,128]{3,1,2,0:T(8,128)(2,1)S(1)}, bf16[2,128,1,128]{3,1,2,0:T(8,128)(2,1)}, u32[]{:S(2)}) copy-start(bf16[2,128,1,128]{3,1,2,0:T(8,128)(2,1)} %param.13) | copy-start | bytes 196612
  9.9 209.6 %all-reduce.3.cloned.1.call-start = ((), (), s32[]{:S(2)}) async-start(), calls=%async_computation.3 | async-start | bytes 983040 | tf_op jit(solution)/shard_map/psum | solution.py:194
  142.4 78.2 %copy-start.1 = (bf16[2,320,1280]{2,1,0:T(8,128)(2,1)S(1)}, bf16[2,320,1280]{2,1,0:T(8,128)(2,1)}, u32[]{:S(2)}) copy-start(bf16[2,320,1280]{2,1,0:T(8,128)(2,1)} %param.14) | copy-start | bytes 4915204
  144.9 149.1 %reduce-scatter.5.cloned.1.call-start = ((), (), s32[]{:S(2)}) async-start(), calls=%async_computation.4 | async-start | bytes 2088960 | tf_op jit(solution)/shard_map/reduce_scatter | solution.py:130
  222.6 205.7 %all-reduce.5.cloned.1.call-start = ((), (), s32[]{:S(2)}) async-start(), calls=%async_computation.5 | async-start | bytes 983040 | tf_op jit(solution)/shard_map/psum | solution.py:194
Sparse Core Ops, SparseCore 0:
  10.2 72.5 reduce-scatter.2
  145.0 74.3 all-reduce.2
  222.7 68.7 reduce-scatter.4
  355.5 72.7 all-reduce.4
where the time goes:
time: 441 us; the launch traced here: 437 us
  blocking collectives  184 us (42%)
  waiting for transfers between devices  147 us (33%)
  matrix products  29.1 us (7%)
  loops' own time  24.4 us (6%)
  local copies, waits for them, and re-layouts  22.9 us (5%)
  other arithmetic  15.6 us (4%)
  between operations  13.5 us (3%)
    psum x2, waiting for transfers between devices, on_device(): update = lax.psum(partial_out, 'tensor')  147 us
    psum x2, blocking collectives, on_device(): total_squares = lax.psum(jnp.sum(stream * stream, axis=1), 'sample')  60.1 us
    all_gather x2, blocking collectives, on_device(): lax.all_gather(keys_here, 'sample', axis=0, tiled=True)  44.5 us
    all_gather x2, blocking collectives, on_device(): lax.all_gather(attention, 'sample', axis=0, tiled=True)  40.9 us
    all_gather x2, blocking collectives, on_device(): lax.all_gather(values_here, 'sample', axis=0, tiled=True)  38.1 us
    another operation x2, loops' own time, fold_prompt(): lax.scan(visit, running, (keys_split, values_split, jnp.arange(block_coun...  24.4 us
    dynamic_slice x32, local copies, waits for them, and re-layouts, fold_prompt(): lax.scan(visit, running, (keys_split, values_split, jnp.arange(block_coun...  21.3 us
    dot_general x32, matrix products, block_stats(): jnp.einsum('rgqd,ngd->rgqn', queries, keys.astype(jnp.float32), precision...  9.63 us
  transfers between devices with their start and end apart: 4, of which 2 were waited for; matrix products, arithmetic and copies ran while one was open for 0% of the time, Pallas kernels for 0%

commit v1 on v0

v1 whole, which is shorter than its diff:
```python
import jax
import jax.numpy as jnp
import numpy as np
from jax import lax
from jax.experimental import pallas as pl
from jax.experimental.pallas import tpu as pltpu
from jax.sharding import PartitionSpec as P

STEPS = 6
NPR = 4
HEADS = 8
HEAD = 128
LAYERS = 2
ROPE_BASE = 1000000.0
EPSILON = 1e-06
NEGATIVE = -1e30
WIDTH = 5120
ROWS = 384
OWN = 24
CHIP = 48
COLS = 320
PAD = 384
PART0 = 640
PART1 = 640
WIDE0 = PART0 + 128
PACKED = 120
COPIES = 128
MESH = pl.DeviceIdType.MESH
F32 = jnp.float32
BF16 = jnp.bfloat16


def dot(a, b):
    return jnp.dot(a, b, preferred_element_type=F32)


def dot_across(a, b):
    return lax.dot_general(a, b, (((1,), (1,)), ((), ())), preferred_element_type=F32)


def iota(shape, axis):
    return lax.broadcasted_iota(jnp.int32, shape, axis)


def pack(block):
    tail = block[:, 256:384]
    low = iota((OWN, 128), 1) < 64
    both = jnp.where(low, tail[:OWN], pltpu.roll(tail[OWN:], 64, 1))
    return jnp.concatenate([block[:, 0:128], block[:, 128:256], both], axis=0)


def unpack_tail(packed):
    both = packed[2 * CHIP :]
    return jnp.concatenate([both, pltpu.roll(both, 64, 1)], axis=0)


def kernel(
    len_ref, freq_ref, hid_hbm, key_hbm, val_hbm, win_hbm, wout_hbm, out_ref,
    hid_across, hid, win, wpad, kv, hs, c0s, c1s, c0r, c1r, s0, s1,
    x0relay, x0dir, x0fin, x1relay, x1dir, x1fin, y1r, y0r,
    q3, low_ref, high_ref, cos_ref, sin_ref, gat, ob, d1r, d2r, sg, fg, str1, out_rows,
    load_sem, send_sem, recv_sem,
):
    s = lax.axis_index("sample")
    z = lax.axis_index("tensor")
    core = s % 2
    chip = s // 2
    x = chip % 4
    y = chip // 4
    other = 1 - y
    sigma = 1 - 2 * core
    ahead = (x + sigma + 4) % 4
    behind = (x - sigma + 4) % 4
    far = (x + 2) % 4
    delta = 2 * ((z + core) % 2) - 1

    def place(py, px, pc):
        return (py * 4 + px) * 2 + pc

    def ring(step):
        return (z + delta * step + 8) % 8

    sibling = {"sample": place(y, x, 1 - core)}
    to_ahead = {"sample": place(y, ahead, core)}
    to_behind = {"sample": place(y, behind, core)}
    to_other = {"sample": place(other, x, core)}
    partner = {"tensor": ring(-1)}

    used = [0]
    pending = []

    def ids(count):
        first = used[0]
        used[0] += count
        return first

    def send(index, src, dst, device):
        copy = pltpu.make_async_remote_copy(
            src_ref=src, dst_ref=dst, send_sem=send_sem.at[index], recv_sem=recv_sem.at[index],
            device_id=device, device_id_type=MESH,
        )
        copy.start()
        pending.append(copy)

    def arrived(index, ref):
        pltpu.make_async_remote_copy(
            src_ref=ref, dst_ref=ref, send_sem=send_sem.at[index], recv_sem=recv_sem.at[index],
            device_id=sibling, device_id_type=MESH,
        ).wait_recv()

    def drain():
        for copy in pending:
            copy.wait_send()
        pending.clear()

    loads = {}

    def load(name, index, src, dst):
        loads[name] = pltpu.make_async_copy(src, dst, load_sem.at[index])
        loads[name].start()

    load("hid", 0, hid_hbm, hid_across.at[pl.ds(0, COLS)])
    load("win0", 1, win_hbm.at[0], win.at[0])
    for layer in range(LAYERS):
        load(("key", layer), 2 + 2 * layer, key_hbm.at[layer], kv.at[layer, s, 0])
        load(("val", layer), 3 + 2 * layer, val_hbm.at[layer], kv.at[layer, s, 1])
    load(("wout", 0), 6, wout_hbm.at[0], wpad.at[0, pl.ds(0, COLS)])
    load("win1", 7, win_hbm.at[1], win.at[1])
    load(("wout", 1), 8, wout_hbm.at[1], wpad.at[1, pl.ds(0, COLS)])
    hid_across[COLS:] = jnp.zeros((PAD - COLS, ROWS), F32)
    for layer in range(LAYERS):
        wpad[layer, COLS:] = jnp.zeros((PAD - COLS, 1024), BF16)

    barrier = pltpu.get_barrier_semaphore()
    near = [sibling, to_ahead, to_behind, to_other]
    near += [{"tensor": ring(step)} for step in (-1, 1, 2, -2, 3)]
    for device in near:
        pl.semaphore_signal(barrier, inc=1, device_id=device, device_id_type=MESH)
    pl.semaphore_wait(barrier, len(near))

    class Gather:
        def __init__(self, buf):
            self.buf = buf
            self.first = ids(15)

        def put(self, number, py, px, device, pc=None):
            block = self.buf.at[place(py, px, core)]
            send(self.first + number, block, block, device)

        def get(self, number, py, px, pc=None):
            where = place(py, px, core if pc is None else pc)
            arrived(self.first + number, self.buf.at[where])

        def begin(self):
            self.put(0, y, x, to_other)
            self.put(1, y, x, to_ahead)
            self.put(2, y, x, to_behind)
            self.put(7, y, x, sibling)

        def cross(self):
            self.get(0, other, x)
            self.put(4, other, x, to_ahead)
            self.put(5, other, x, to_behind)
            self.put(11, other, x, sibling)

        def along(self, half):
            py, at, near_core = (y, 1, 8) if half == 0 else (other, 4, 12)
            self.get(at, py, behind)
            self.put(at + 2, py, behind, to_ahead)
            self.put(near_core, py, behind, sibling)
            self.get(at + 1, py, ahead)
            self.put(near_core + 1, py, ahead, sibling)

        def last(self, half):
            py, at, near_core = (y, 3, 10) if half == 0 else (other, 6, 14)
            self.get(at, py, far)
            self.put(near_core, py, far, sibling)

        def core_side(self, half):
            py, at = (y, 7) if half == 0 else (other, 11)
            for number, px in enumerate((x, ahead, behind, far)):
                self.get(at + number, py, px, 1 - core)

    gathers = [Gather(kv.at[layer]) for layer in range(LAYERS)]
    loads[("key", 0)].wait()
    loads[("val", 0)].wait()
    gathers[0].begin()

    loads["hid"].wait()
    hid[...] = hid_across[...].T
    for parity in range(2):
        pieces = [hid[CHIP * q + OWN * parity : CHIP * q + OWN * parity + OWN, :COLS] for q in range(8)]
        hs[parity] = jnp.concatenate(pieces, axis=0).astype(BF16)
        for q in range(8):
            squares = jnp.sum(pieces[q] * pieces[q], axis=1, keepdims=True)
            target = s0.at[q % 4, q // 4] if parity == 0 else c0s.at[q % 4, q // 4]
            target[:, PART0:] = jnp.broadcast_to(squares, (OWN, 128))
    flip = core == 1
    for q in range(8):
        zero_rows = s0[q % 4, q // 4, :, PART0:]
        one_rows = c0s[q % 4, q // 4, :, PART0:]
        s0[q % 4, q // 4, :, PART0:] = jnp.where(flip, one_rows, zero_rows)
        c0s[q % 4, q // 4, :, PART0:] = jnp.where(flip, zero_rows, one_rows)
    loads["win0"].wait()

    def tables():
        row = iota((OWN, 128), 0)
        lane = iota((OWN, 128), 1)
        prompt = lax.shift_right_logical(row * 43, 8)
        step = row - prompt * STEPS
        length = jnp.zeros((OWN, 128), jnp.int32)
        start = jnp.zeros((OWN, 128), jnp.int32)
        offset = jnp.int32(0)
        for k in range(NPR):
            length = jnp.where(prompt == k, len_ref[k], length)
            start = jnp.where(prompt == k, offset, start)
            offset = offset + len_ref[k]
        low_ref[...] = start - lane
        high_ref[...] = start + length - lane
        angle = (length + step).astype(F32) * freq_ref[...]
        cos_ref[...] = jnp.cos(angle)
        sin_ref[...] = jnp.where(lane < 64, -jnp.sin(angle), jnp.sin(angle))

    def project(layer):
        first = ids(14)
        sib = hs[1 - core]
        weights = win.at[layer]
        part = dot(sib, weights[:, PART0:])
        c1s[...] = part.reshape(2, 4, OWN, PART1)
        send(first + 0, c1s.at[other], c1r.at[layer, other], sibling)
        part = dot(sib, weights[:, :PART0])
        for q in range(8):
            c0s[q % 4, q // 4, :, :PART0] = part[OWN * q : OWN * q + OWN]
        send(first + 1, c0s.at[far], c0r.at[layer, far], sibling)
        send(first + 2, c0s.at[ahead], c0r.at[layer, ahead], sibling)
        send(first + 3, c0s.at[behind], c0r.at[layer, behind], sibling)
        send(first + 4, c0s.at[x], c0r.at[layer, x], sibling)
        send(first + 5, c1s.at[y], c1r.at[layer, y], sibling)
        mine = hs[core]
        part = dot(mine, weights[:, PART0:])
        s1[...] = part.reshape(2, 4, OWN, PART1)
        part = dot(mine, weights[:, :PART0])
        for q in range(8):
            s0[q % 4, q // 4, :, :PART0] = part[OWN * q : OWN * q + OWN]

        def core_sum(index, total, came):
            arrived(index, came)
            total[...] = total[...] + came[...]

        core_sum(first + 0, s1.at[other], c1r.at[layer, other])
        send(first + 6, s1.at[other], y1r.at[layer], to_other)
        core_sum(first + 1, s0.at[far], c0r.at[layer, far])
        send(first + 7, s0.at[far], x0relay.at[layer], to_ahead)
        core_sum(first + 2, s0.at[behind], c0r.at[layer, behind])
        send(first + 8, s0.at[behind], x0dir.at[layer], to_behind)
        core_sum(first + 3, s0.at[ahead], c0r.at[layer, ahead])
        core_sum(first + 4, s0.at[x], c0r.at[layer, x])
        core_sum(first + 5, s1.at[y], c1r.at[layer, y])
        if layer == 0:
            gathers[0].cross()
            gathers[0].along(0)
            tables()
        arrived(first + 7, x0relay.at[layer])
        s0[ahead] = s0[ahead] + x0relay[layer]
        send(first + 9, s0.at[ahead], x0fin.at[layer], to_ahead)
        arrived(first + 6, y1r.at[layer])
        s1[y] = s1[y] + y1r[layer]
        send(first + 10, s1.at[y, far], x1relay.at[layer], to_ahead)
        send(first + 11, s1.at[y, behind], x1dir.at[layer], to_behind)
        if layer == 0:
            gathers[0].last(0)
            gathers[0].along(1)
        arrived(first + 10, x1relay.at[layer])
        s1[y, ahead] = s1[y, ahead] + x1relay[layer]
        send(first + 12, s1.at[y, ahead], x1fin.at[layer], to_ahead)
        arrived(first + 8, x0dir.at[layer])
        arrived(first + 9, x0fin.at[layer])
        s0[x] = s0[x] + x0dir[layer] + x0fin[layer]
        send(first + 13, s0.at[x, other], y0r.at[layer], to_other)
        if layer == 0:
            gathers[0].last(1)
            gathers[0].core_side(0)
            gathers[0].core_side(1)
        arrived(first + 11, x1dir.at[layer])
        arrived(first + 12, x1fin.at[layer])
        part1 = s1[y, x] + x1dir[layer] + x1fin[layer]
        arrived(first + 13, y0r.at[layer])
        part0 = s0[x, y] + y0r[layer]
        return part0, part1

    def attend(layer, part0, part1):
        inverse = lax.rsqrt(part0[:, PART0:] / WIDTH + EPSILON)
        cosine = cos_ref[...]
        sine = sin_ref[...]

        def rotate(vector):
            return vector * cosine + pltpu.roll(vector, 64, 1) * sine

        blocks = [part0[:, HEAD * h : HEAD * h + HEAD] * inverse for h in range(5)]
        blocks += [part1[:, HEAD * h : HEAD * h + HEAD] * inverse for h in range(5)]
        queries = jnp.concatenate([rotate(block) for block in blocks[:HEADS]], axis=0)
        rows = HEADS * OWN
        first = queries.astype(BF16)
        rest = queries - first.astype(F32)
        second = rest.astype(BF16)
        third = (rest - second.astype(F32)).astype(BF16)
        q3[0:rows] = first
        q3[rows : 2 * rows] = second
        q3[2 * rows :] = third
        empty = jnp.zeros((128 - OWN, HEAD), F32)
        kv[layer, 16, 0] = jnp.concatenate([rotate(blocks[8]), empty], axis=0).astype(BF16)
        kv[layer, 16, 1] = jnp.concatenate([blocks[9], empty], axis=0).astype(BF16)

        def visit(block, seen, running):
            peak, total, summed = running
            scores = dot_across(q3[...], kv[layer, block, 0])
            scores = (scores[2 * rows :] + scores[rows : 2 * rows]) + scores[:rows]
            bias = jnp.where(seen, 0.0, NEGATIVE)
            factor = jnp.where(seen, 1.0, 0.0)
            scores = (scores * HEAD**-0.5).reshape(HEADS, OWN, 128) + bias[None]
            maxima = jnp.max(scores, axis=-1, keepdims=True)
            weights = jnp.exp(scores - maxima) * factor[None]
            sums = jnp.sum(weights, axis=-1, keepdims=True)
            values = dot(weights.reshape(rows, 128).astype(BF16), kv[layer, block, 1])
            higher = jnp.maximum(peak, maxima)
            left = jnp.exp(peak - higher)
            right = jnp.exp(maxima - higher)
            return (
                higher,
                total * left + sums * right,
                summed * left + values.reshape(HEADS, OWN, HEAD) * right,
            )

        def prompt_block(block, running):
            at = block * 128
            seen = (low_ref[...] <= at) & (high_ref[...] > at)
            return visit(block, seen, running)

        running = (
            jnp.full((HEADS, OWN, 1), NEGATIVE, F32),
            jnp.zeros((HEADS, OWN, 1), F32),
            jnp.zeros((HEADS, OWN, HEAD), F32),
        )
        running = lax.fori_loop(0, 16, prompt_block, running, unroll=2)
        row = iota((OWN, 128), 0)
        lane = iota((OWN, 128), 1)
        row_sample = lax.shift_right_logical(row * 43, 8)
        lane_sample = lax.shift_right_logical(lane * 43, 8)
        recent = (row_sample == lane_sample) & (lane <= row)
        _, total, summed = visit(16, recent, running)
        attention = summed / total
        top = jnp.concatenate([attention[h] for h in range(4)], axis=1)
        bottom = jnp.concatenate([attention[h] for h in range(4, 8)], axis=1)
        gat[layer, s] = jnp.concatenate([top, bottom], axis=0).astype(BF16)

    def collect(layer):
        gather = Gather(gat.at[layer])
        gather.begin()
        gather.cross()
        gather.along(0)
        gather.along(1)
        gather.last(0)
        gather.last(1)

        def product(half):
            rows = gat[layer, pl.ds(half * 8, 8)].reshape(8 * CHIP, 512)
            upper = dot_across(rows, wpad[layer, :, :512])
            lower = dot_across(rows, wpad[layer, :, 512:])
            for q in range(4):
                at = 2 * CHIP * q
                block = jnp.concatenate(
                    [
                        upper[at : at + OWN] + lower[at + OWN : at + CHIP],
                        upper[at + CHIP : at + CHIP + OWN] + lower[at + CHIP + OWN : at + 2 * CHIP],
                    ],
                    axis=0,
                )
                ob[half * 4 + q] = pack(block)

        loads[("wout", layer)].wait()
        gather.core_side(0)
        product(y)
        gather.core_side(1)
        product(other)

    def tensor_sum(layer):
        first = ids(7)
        for k in (3, 2, 1, 0):
            send(first + k, ob.at[ring(-1 - k)], d1r.at[layer, k], partner)
        if layer == 0:
            loads[("key", 1)].wait()
            loads[("val", 1)].wait()
            gathers[1].begin()
        for k in (3, 2, 1):
            at = ring(k)
            arrived(first + k, d1r.at[layer, k])
            ob[at] = ob[at] + d1r[layer, k]
            send(first + 3 + k, ob.at[at], d2r.at[layer, k - 1], {"tensor": at})
        arrived(first + 0, d1r.at[layer, 0])
        total = ob[z] + d1r[layer, 0]
        if layer == 0:
            gathers[1].cross()
            gathers[1].along(0)
        for k in (1, 2, 3):
            arrived(first + 3 + k, d2r.at[layer, k - 1])
            total = total + d2r[layer, k - 1]
        return total

    def tensor_gather(buf):
        first = ids(7)
        mine = buf.at[z]
        send(first + 2, mine, mine, {"tensor": ring(3)})
        send(first + 1, mine, mine, {"tensor": ring(-2)})
        send(first + 0, mine, mine, {"tensor": ring(1)})
        send(first + 3, mine, mine, partner)
        for k in (1, 2, 3):
            block = buf.at[ring(k)]
            arrived(first + k - 1, block)
            send(first + 3 + k, block, block, partner)
        for k in (0, 1, 2, 3):
            arrived(first + 3 + k, buf.at[ring(-1 - k)])

    part0, part1 = project(0)
    attend(0, part0, part1)
    collect(0)
    stream = pack(hid[pl.ds(pl.multiple_of(z * CHIP, 8), CHIP), :]) + tensor_sum(0)
    str1[...] = stream
    tail = unpack_tail(stream)
    lane = iota((CHIP, 128), 1)
    middle0 = stream[:CHIP]
    middle1 = stream[CHIP : 2 * CHIP]
    kept = jnp.where(lane < 64, tail, 0.0)
    squares = jnp.sum(middle0 * middle0 + middle1 * middle1 + kept * kept, axis=1, keepdims=True)
    square1 = squares.astype(BF16).astype(F32)
    square2 = (squares - square1).astype(BF16).astype(F32)
    square3 = squares - square1 - square2
    kept = jnp.where(lane == 64, square1, kept)
    kept = jnp.where(lane == 65, square2, kept)
    kept = jnp.where(lane == 66, square3, kept)
    sg[z] = jnp.concatenate([middle0, middle1, kept], axis=1).astype(BF16)
    tensor_gather(sg)
    gathers[1].last(0)
    gathers[1].along(1)
    drain()

    flip = core == 1
    by_parity = [[], []]
    for q in range(8):
        block = sg[q].astype(F32)
        sums = jnp.sum(jnp.where(lane >= 64, block[:, 256:], 0.0), axis=1, keepdims=True)
        sums = jnp.broadcast_to(sums, (CHIP, 128))
        s0[q % 4, q // 4, :, PART0:] = jnp.where(flip, sums[OWN:], sums[:OWN])
        c0s[q % 4, q // 4, :, PART0:] = jnp.where(flip, sums[:OWN], sums[OWN:])
        for parity in range(2):
            by_parity[parity].append(block[OWN * parity : OWN * parity + OWN, :COLS])
    for parity in range(2):
        hs[parity] = jnp.concatenate(by_parity[parity], axis=0).astype(BF16)
    loads["win1"].wait()
    part0, part1 = project(1)
    gathers[1].last(1)
    gathers[1].core_side(0)
    gathers[1].core_side(1)
    attend(1, part0, part1)
    collect(1)
    fg[z] = str1[...] + tensor_sum(1)
    tensor_gather(fg)
    for d in range(8):
        block = fg[d]
        rows = slice(CHIP * d, CHIP * d + CHIP)
        out_rows[rows, 0:128] = block[:CHIP]
        out_rows[rows, 128:256] = block[CHIP : 2 * CHIP]
        out_rows[rows, 256:384] = unpack_tail(block)
    out_ref[...] = out_rows[...].T[:COLS]
    drain()


def on_device(hidden_in, prompt_len, cached_prompt_keys, cached_prompt_values, query_key_value_weight, w_out):
    keys = cached_prompt_keys.reshape(LAYERS, 128, HEAD)
    values = cached_prompt_values.reshape(LAYERS, 128, HEAD)
    half = np.power(ROPE_BASE, -2.0 * np.arange(64) / HEAD)
    freq = jnp.asarray(np.concatenate([half, half])[None, :], F32)
    vmem = pltpu.VMEM
    scratch = [
        vmem((PAD, ROWS), F32),
        vmem((ROWS, PAD), F32),
        vmem((LAYERS, COLS, 1280), BF16),
        vmem((LAYERS, PAD, 1024), BF16),
        vmem((LAYERS, 17, 2, 128, HEAD), BF16),
        vmem((2, 192, COLS), BF16),
        vmem((4, 2, OWN, WIDE0), F32),
        vmem((2, 4, OWN, PART1), F32),
        vmem((LAYERS, 4, 2, OWN, WIDE0), F32),
        vmem((LAYERS, 2, 4, OWN, PART1), F32),
        vmem((4, 2, OWN, WIDE0), F32),
        vmem((2, 4, OWN, PART1), F32),
        vmem((LAYERS, 2, OWN, WIDE0), F32),
        vmem((LAYERS, 2, OWN, WIDE0), F32),
        vmem((LAYERS, 2, OWN, WIDE0), F32),
        vmem((LAYERS, OWN, PART1), F32),
        vmem((LAYERS, OWN, PART1), F32),
        vmem((LAYERS, OWN, PART1), F32),
        vmem((LAYERS, 4, OWN, PART1), F32),
        vmem((LAYERS, OWN, WIDE0), F32),
        vmem((3 * HEADS * OWN, HEAD), BF16),
        vmem((OWN, 128), jnp.int32),
        vmem((OWN, 128), jnp.int32),
        vmem((OWN, 128), F32),
        vmem((OWN, 128), F32),
        vmem((LAYERS, 16, CHIP, 512), BF16),
        vmem((8, PACKED, 128), F32),
        vmem((LAYERS, 4, PACKED, 128), F32),
        vmem((LAYERS, 3, PACKED, 128), F32),
        vmem((8, CHIP, PAD), BF16),
        vmem((8, PACKED, 128), F32),
        vmem((PACKED, 128), F32),
        vmem((ROWS, PAD), F32),
        pltpu.SemaphoreType.DMA((9,)),
        pltpu.SemaphoreType.DMA((COPIES,)),
        pltpu.SemaphoreType.DMA((COPIES,)),
    ]
    hbm = pl.BlockSpec(memory_space=pl.ANY)
    out = pl.pallas_call(
        kernel,
        out_shape=jax.ShapeDtypeStruct((COLS, ROWS), F32),
        in_specs=[
            pl.BlockSpec(memory_space=pltpu.SMEM),
            pl.BlockSpec(memory_space=pltpu.VMEM),
            hbm, hbm, hbm, hbm, hbm,
        ],
        out_specs=pl.BlockSpec(memory_space=pltpu.VMEM),
        scratch_shapes=scratch,
        compiler_params=pltpu.CompilerParams(
            collective_id=0, has_side_effects=True, vmem_limit_bytes=60 * 1024 * 1024
        ),
        name="two_layers",
    )(prompt_len, freq, hidden_in.T, keys, values, query_key_value_weight, w_out.transpose(0, 2, 1))
    return out.T


def solution(mesh):
    return jax.shard_map(
        on_device,
        mesh=mesh,
        in_specs=(
            P("prompt", "sample"),
            P("prompt"),
            P(None, ("prompt", "sample"), "tensor", None),
            P(None, ("prompt", "sample"), "tensor", None),
            P(None, "sample", "tensor"),
            P(None, "tensor", "sample"),
        ),
        out_specs=P("prompt", "sample"),
        check_vma=False,
    )
```

time: 441 us -> 127 us (0.29)
  blocking collectives: 184 us -> 0 us
  waiting for transfers between devices: 147 us -> 0 us
  Pallas kernels: 0 us -> 125 us
  matrix products: 29.1 us -> 0 us
  loops' own time: 24.4 us -> 0 us
  local copies, waits for them, and re-layouts: 22.9 us -> 1.84 us
  other arithmetic: 15.6 us -> 0 us
  between operations: 13.5 us -> 0.01 us
    psum x2 -> x0, waiting for transfers between devices: 147 us -> none  [on_device(): update = lax.psum(partial_out, 'tensor')]
    pallas_call x0 -> x1, Pallas kernels: none -> 125 us  [on_device(): pl.pallas_call(kernel, out_shape=jax.ShapeDtypeStruct((COLS, ROWS), F32),...]
    all_gather x6 -> x0, blocking collectives: 123 us -> none  [the longest x2 44.5 us: on_device(): lax.all_gather(keys_here, 'sample', axis=0, tiled=True)]
    psum x2 -> x0, blocking collectives: 60.1 us -> none  [on_device(): total_squares = lax.psum(jnp.sum(stream * stream, axis=1), 'sample')]
    dot_general x72 -> x0, matrix products: 29.1 us -> none  [the longest x32 9.63 us: block_stats(): jnp.einsum('rgqd,ngd->rgqn', queries, keys.astype(jnp.float32), precision...]
    another operation x2 -> x0, loops' own time: 24.4 us -> none  [fold_prompt(): lax.scan(visit, running, (keys_split, values_split, jnp.arange(block_coun...]
    dynamic_slice x37 -> x0, local copies, waits for them, and re-layouts: 21.7 us -> none  [the longest x32 21.3 us: fold_prompt(): lax.scan(visit, running, (keys_split, values_split, jnp.arange(block_coun...]
    reduce_sum x37 -> x0, other arithmetic: 7.18 us -> none  [the longest x34 5.91 us: softmax_parts(): totals = jnp.sum(weights, axis=-1)]
  transfers between devices with their start and end apart: 4 -> 0, of which waited for: 2 -> 0; matrix products, arithmetic and copies ran while one was open for 0% -> 0% of each run, Pallas kernels for 0% -> 0%
where the time goes in v1:
time: 127 us
  Pallas kernels  125 us (98%)
  local copies, waits for them, and re-layouts  1.84 us (1%)
    pallas_call x1, Pallas kernels, on_device(): pl.pallas_call(kernel, out_shape=jax.ShapeDtypeStruct((COLS, ROWS), F32),...  125 us

profile of v1, /device:TPU:1, one launch (start us, length us, event | category | flops | bytes accessed | tf_op | source)
XLA Modules:
  0.0 126.6 jit_solution(11358847743597098876)
XLA Ops:
  0.0 124.7 %two_layers.1 = f32[320,384]{1,0:T(8,128)} custom-call(s32[4]{0:T(128)} %len_ref.1, f32[1,128]{1,0:T(1,128)} %constant.2.clone.freq_ref, f32[320,384]{1,0:T(8,128)} %bitcast.7, bf16[2,128,128]{2,1,0:T(8,128)(2,1)} %bitcast.8, bf16[2,128,128]{2,1,0:T(8,128)(2,1)} %bitcast.9, bf16[2,320,1280]{2,1,0:T(8,128)(2,1)} %win_hbm.1, bf16[2,320,1024]{2,1,0:T(8,128)(2,1)} %bitcast.6), custom_call_target="tpu_custom_call" | custom-call | tf_op jit(solution)/shard_map/two_layers/pallas_call | solution.py:522
  124.8 1.8 %copy.9 = f32[384,320]{0,1:T(8,128)} copy(f32[384,320]{0,1:T(8,128)} %bitcast.5) | data formatting | bytes 983040

commit v2 on v1

--- a/solution.py
+++ b/solution.py
@@ -34,10 +34,6 @@
     return jnp.dot(a, b, preferred_element_type=F32)
 
 
-def dot_across(a, b):
-    return lax.dot_general(a, b, (((1,), (1,)), ((), ())), preferred_element_type=F32)
-
-
 def iota(shape, axis):
     return lax.broadcasted_iota(jnp.int32, shape, axis)
 
@@ -56,9 +52,9 @@
 
 def kernel(
     len_ref, freq_ref, hid_hbm, key_hbm, val_hbm, win_hbm, wout_hbm, out_ref,
-    hid_across, hid, win, wpad, kv, hs, c0s, c1s, c0r, c1r, s0, s1,
+    hid_across, hid, win, wpad, wout, val, kv, hs, c0s, c1s, c0r, c1r, s0, s1,
     x0relay, x0dir, x0fin, x1relay, x1dir, x1fin, y1r, y0r,
-    q3, low_ref, high_ref, cos_ref, sin_ref, gat, ob, d1r, d2r, sg, fg, str1, out_rows,
+    past_ref, length_ref, cos_ref, sin_ref, gat, ob, d1r, d2r, sg, fg, str1, out_rows,
     load_sem, send_sem, recv_sem,
 ):
     s = lax.axis_index("sample")
@@ -80,6 +76,9 @@
     def ring(step):
         return (z + delta * step + 8) % 8
 
+    def chip_of(at):
+        return (at % 2) * 4 + at // 2
+
     sibling = {"sample": place(y, x, 1 - core)}
     to_ahead = {"sample": place(y, ahead, core)}
     to_behind = {"sample": place(y, behind, core)}
@@ -123,7 +122,7 @@
     load("win0", 1, win_hbm.at[0], win.at[0])
     for layer in range(LAYERS):
         load(("key", layer), 2 + 2 * layer, key_hbm.at[layer], kv.at[layer, s, 0])
-        load(("val", layer), 3 + 2 * layer, val_hbm.at[layer], kv.at[layer, s, 1])
+        load(("val", layer), 3 + 2 * layer, val_hbm.at[layer], val.at[layer])
     load(("wout", 0), 6, wout_hbm.at[0], wpad.at[0, pl.ds(0, COLS)])
     load("win1", 7, win_hbm.at[1], win.at[1])
     load(("wout", 1), 8, wout_hbm.at[1], wpad.at[1, pl.ds(0, COLS)])
@@ -182,9 +181,14 @@
                 self.get(at + number, py, px, 1 - core)
 
     gathers = [Gather(kv.at[layer]) for layer in range(LAYERS)]
-    loads[("key", 0)].wait()
-    loads[("val", 0)].wait()
-    gathers[0].begin()
+
+    def begin_prompt(layer):
+        loads[("key", layer)].wait()
+        loads[("val", layer)].wait()
+        kv[layer, s, 1] = val[layer].astype(F32).T.astype(BF16)
+        gathers[layer].begin()
+
+    begin_prompt(0)
 
     loads["hid"].wait()
     hid[...] = hid_across[...].T
@@ -209,17 +213,24 @@
         prompt = lax.shift_right_logical(row * 43, 8)
         step = row - prompt * STEPS
         length = jnp.zeros((OWN, 128), jnp.int32)
-        start = jnp.zeros((OWN, 128), jnp.int32)
+        for k in range(NPR):
+            length = jnp.where(prompt == k, len_ref[k], length)
+        angle = (length + step).astype(F32) * freq_ref[...]
+        cos_ref[...] = jnp.cos(angle)
+        sin_ref[...] = jnp.where(lane < 64, -jnp.sin(angle), jnp.sin(angle))
+        key = iota((128, 128), 0)
+        query = iota((128, 128), 1)
+        query_row = query - lax.shift_right_logical(query * 171, 12) * OWN
+        prompt = lax.shift_right_logical(query_row * 43, 8)
+        length = jnp.zeros((128, 128), jnp.int32)
+        start = jnp.zeros((128, 128), jnp.int32)
         offset = jnp.int32(0)
         for k in range(NPR):
             length = jnp.where(prompt == k, len_ref[k], length)
             start = jnp.where(prompt == k, offset, start)
             offset = offset + len_ref[k]
-        low_ref[...] = start - lane
-        high_ref[...] = start + length - lane
-        angle = (length + step).astype(F32) * freq_ref[...]
-        cos_ref[...] = jnp.cos(angle)
-        sin_ref[...] = jnp.where(lane < 64, -jnp.sin(angle), jnp.sin(angle))
+        past_ref[...] = key - start
+        length_ref[...] = length
 
     def project(layer):
         first = ids(14)
@@ -260,6 +271,8 @@
             gathers[0].cross()
             gathers[0].along(0)
             tables()
+        loads[("wout", layer)].wait()
+        wout[...] = wpad[layer].T
         arrived(first + 7, x0relay.at[layer])
         s0[ahead] = s0[ahead] + x0relay[layer]
         send(first + 9, s0.at[ahead], x0fin.at[layer], to_ahead)
@@ -298,74 +311,83 @@
 
         blocks = [part0[:, HEAD * h : HEAD * h + HEAD] * inverse for h in range(5)]
         blocks += [part1[:, HEAD * h : HEAD * h + HEAD] * inverse for h in range(5)]
-        queries = jnp.concatenate([rotate(block) for block in blocks[:HEADS]], axis=0)
-        rows = HEADS * OWN
+        spare = jnp.zeros((128 - 4 * OWN, HEAD), F32)
+        queries = [rotate(block) * HEAD**-0.5 for block in blocks[:HEADS]]
+        queries = [jnp.concatenate(queries[4 * half : 4 * half + 4] + [spare], axis=0).T for half in range(2)]
+        queries = jnp.concatenate(queries, axis=1)
         first = queries.astype(BF16)
         rest = queries - first.astype(F32)
         second = rest.astype(BF16)
         third = (rest - second.astype(F32)).astype(BF16)
-        q3[0:rows] = first
-        q3[rows : 2 * rows] = second
-        q3[2 * rows :] = third
+        upper = jnp.concatenate([first, second], axis=0)
         empty = jnp.zeros((128 - OWN, HEAD), F32)
         kv[layer, 16, 0] = jnp.concatenate([rotate(blocks[8]), empty], axis=0).astype(BF16)
-        kv[layer, 16, 1] = jnp.concatenate([blocks[9], empty], axis=0).astype(BF16)
-
-        def visit(block, seen, running):
+        kv[layer, 16, 1] = jnp.concatenate([blocks[9], empty], axis=0).T.astype(BF16)
+
+        def visit(block, count, seen, running):
             peak, total, summed = running
-            scores = dot_across(q3[...], kv[layer, block, 0])
-            scores = (scores[2 * rows :] + scores[rows : 2 * rows]) + scores[:rows]
-            bias = jnp.where(seen, 0.0, NEGATIVE)
-            factor = jnp.where(seen, 1.0, 0.0)
-            scores = (scores * HEAD**-0.5).reshape(HEADS, OWN, 128) + bias[None]
-            maxima = jnp.max(scores, axis=-1, keepdims=True)
-            weights = jnp.exp(scores - maxima) * factor[None]
-            sums = jnp.sum(weights, axis=-1, keepdims=True)
-            values = dot(weights.reshape(rows, 128).astype(BF16), kv[layer, block, 1])
-            higher = jnp.maximum(peak, maxima)
+            keys = kv[layer, pl.ds(block, count), 0].reshape(count * 128, HEAD)
+            scores = dot(keys, third) + dot(jnp.concatenate([keys, keys], axis=1), upper)
+            parts = []
+            for i in range(count):
+                bias = jnp.where(seen(i), 0.0, NEGATIVE)
+                part = scores[128 * i : 128 * i + 128] + jnp.concatenate([bias, bias], axis=1)
+                maxima = jnp.max(part, axis=0, keepdims=True)
+                weights = jnp.exp(part - maxima)
+                sums = jnp.sum(weights, axis=0, keepdims=True)
+                parts.append((maxima, sums, dot(kv[layer, block + i, 1], weights.astype(BF16))))
+            higher = peak
+            for maxima, _, _ in parts:
+                higher = jnp.maximum(higher, maxima)
             left = jnp.exp(peak - higher)
-            right = jnp.exp(maxima - higher)
-            return (
-                higher,
-                total * left + sums * right,
-                summed * left + values.reshape(HEADS, OWN, HEAD) * right,
-            )
-
-        def prompt_block(block, running):
-            at = block * 128
-            seen = (low_ref[...] <= at) & (high_ref[...] > at)
-            return visit(block, seen, running)
-
+            total = total * left
+            summed = summed * left
+            for maxima, sums, values in parts:
+                right = jnp.exp(maxima - higher)
+                total = total + sums * right
+                summed = summed + values * right
+            return higher, total, summed
+
+        key = iota((128, 128), 0)
+        query = iota((128, 128), 1)
+        query_row = query - lax.shift_right_logical(query * 171, 12) * OWN
+        query_sample = lax.shift_right_logical(query_row * 43, 8)
+        key_sample = lax.shift_right_logical(key * 43, 8)
+        recent = (query_sample == key_sample) & (key <= query_row)
         running = (
-            jnp.full((HEADS, OWN, 1), NEGATIVE, F32),
-            jnp.zeros((HEADS, OWN, 1), F32),
-            jnp.zeros((HEADS, OWN, HEAD), F32),
+            jnp.full((1, 256), NEGATIVE, F32),
+            jnp.zeros((1, 256), F32),
+            jnp.zeros((HEAD, 256), F32),
         )
-        running = lax.fori_loop(0, 16, prompt_block, running, unroll=2)
-        row = iota((OWN, 128), 0)
-        lane = iota((OWN, 128), 1)
-        row_sample = lax.shift_right_logical(row * 43, 8)
-        lane_sample = lax.shift_right_logical(lane * 43, 8)
-        recent = (row_sample == lane_sample) & (lane <= row)
-        _, total, summed = visit(16, recent, running)
+        running = visit(16, 1, lambda i: recent, running)
+
+        def prompt_blocks(group, running):
+            def seen(i):
+                past = past_ref[...] + (group * 4 + i) * 128
+                return (past >= 0) & (past < length_ref[...])
+
+            return visit(group * 4, 4, seen, running)
+
+        _, total, summed = lax.fori_loop(0, 4, prompt_blocks, running)
         attention = summed / total
-        top = jnp.concatenate([attention[h] for h in range(4)], axis=1)
-        bottom = jnp.concatenate([attention[h] for h in range(4, 8)], axis=1)
-        gat[layer, s] = jnp.concatenate([top, bottom], axis=0).astype(BF16)
+        halves = []
+        for half in range(2):
+            rows = attention[:, 128 * half : 128 * half + 128].T
+            halves.append(jnp.concatenate([rows[OWN * h : OWN * h + OWN] for h in range(4)], axis=1))
+        gat[layer, s] = jnp.concatenate(halves, axis=0).astype(BF16)
 
     def collect(layer):
         gather = Gather(gat.at[layer])
         gather.begin()
+        gather.along(0)
         gather.cross()
-        gather.along(0)
+        gather.last(0)
         gather.along(1)
-        gather.last(0)
-        gather.last(1)
 
         def product(half):
             rows = gat[layer, pl.ds(half * 8, 8)].reshape(8 * CHIP, 512)
-            upper = dot_across(rows, wpad[layer, :, :512])
-            lower = dot_across(rows, wpad[layer, :, 512:])
+            upper = dot(rows, wout[:512])
+            lower = dot(rows, wout[512:])
             for q in range(4):
                 at = 2 * CHIP * q
                 block = jnp.concatenate(
@@ -377,27 +399,31 @@
                 )
                 ob[half * 4 + q] = pack(block)
 
-        loads[("wout", layer)].wait()
+        first = ids(7)
+        early = (y + z + 1) % 2
+
+        def hand_over(k):
+            send(first + k, ob.at[chip_of(ring(-1 - k))], d1r.at[layer, k], partner)
+
         gather.core_side(0)
         product(y)
+        hand_over(early + 2)
+        hand_over(early)
+        gather.last(1)
         gather.core_side(1)
         product(other)
-
-    def tensor_sum(layer):
-        first = ids(7)
-        for k in (3, 2, 1, 0):
-            send(first + k, ob.at[ring(-1 - k)], d1r.at[layer, k], partner)
+        hand_over(3 - early)
+        hand_over(1 - early)
         if layer == 0:
-            loads[("key", 1)].wait()
-            loads[("val", 1)].wait()
-            gathers[1].begin()
-        for k in (3, 2, 1):
+            begin_prompt(1)
+        for k in (early + 2, 3 - early, 1):
             at = ring(k)
+            block = ob.at[chip_of(at)]
             arrived(first + k, d1r.at[layer, k])
-            ob[at] = ob[at] + d1r[layer, k]
-            send(first + 3 + k, ob.at[at], d2r.at[layer, k - 1], {"tensor": at})
+            block[...] = block[...] + d1r[layer, k]
+            send(first + 3 + k, block, d2r.at[layer, k - 1], {"tensor": at})
         arrived(first + 0, d1r.at[layer, 0])
-        total = ob[z] + d1r[layer, 0]
+        total = ob[chip_of(z)] + d1r[layer, 0]
         if layer == 0:
             gathers[1].cross()
             gathers[1].along(0)
@@ -422,8 +448,7 @@
 
     part0, part1 = project(0)
     attend(0, part0, part1)
-    collect(0)
-    stream = pack(hid[pl.ds(pl.multiple_of(z * CHIP, 8), CHIP), :]) + tensor_sum(0)
+    stream = pack(hid[pl.ds(pl.multiple_of(chip_of(z) * CHIP, 8), CHIP), :]) + collect(0)
     str1[...] = stream
     tail = unpack_tail(stream)
     lane = iota((CHIP, 128), 1)
@@ -446,7 +471,7 @@
     flip = core == 1
     by_parity = [[], []]
     for q in range(8):
-        block = sg[q].astype(F32)
+        block = sg[2 * (q % 4) + q // 4].astype(F32)
         sums = jnp.sum(jnp.where(lane >= 64, block[:, 256:], 0.0), axis=1, keepdims=True)
         sums = jnp.broadcast_to(sums, (CHIP, 128))
         s0[q % 4, q // 4, :, PART0:] = jnp.where(flip, sums[OWN:], sums[:OWN])
@@ -461,12 +486,11 @@
     gathers[1].core_side(0)
     gathers[1].core_side(1)
     attend(1, part0, part1)
-    collect(1)
-    fg[z] = str1[...] + tensor_sum(1)
+    fg[z] = str1[...] + collect(1)
     tensor_gather(fg)
     for d in range(8):
         block = fg[d]
-        rows = slice(CHIP * d, CHIP * d + CHIP)
+        rows = pl.ds(CHIP * chip_of(d), CHIP)
         out_rows[rows, 0:128] = block[:CHIP]
         out_rows[rows, 128:256] = block[CHIP : 2 * CHIP]
         out_rows[rows, 256:384] = unpack_tail(block)
@@ -485,6 +509,8 @@
         vmem((ROWS, PAD), F32),
         vmem((LAYERS, COLS, 1280), BF16),
         vmem((LAYERS, PAD, 1024), BF16),
+        vmem((1024, PAD), BF16),
+        vmem((LAYERS, 128, HEAD), BF16),
         vmem((LAYERS, 17, 2, 128, HEAD), BF16),
         vmem((2, 192, COLS), BF16),
         vmem((4, 2, OWN, WIDE0), F32),
@@ -501,9 +527,8 @@
         vmem((LAYERS, OWN, PART1), F32),
         vmem((LAYERS, 4, OWN, PART1), F32),
         vmem((LAYERS, OWN, WIDE0), F32),
-        vmem((3 * HEADS * OWN, HEAD), BF16),
-        vmem((OWN, 128), jnp.int32),
-        vmem((OWN, 128), jnp.int32),
+        vmem((128, 128), jnp.int32),
+        vmem((128, 128), jnp.int32),
         vmem((OWN, 128), F32),
         vmem((OWN, 128), F32),
         vmem((LAYERS, 16, CHIP, 512), BF16),

time: 127 us -> 122 us (0.961)
  Pallas kernels: 125 us -> 120 us
    pallas_call x1, Pallas kernels: 125 us -> 120 us  [on_device(): pl.pallas_call(kernel, out_shape=jax.ShapeDtypeStruct((COLS, ROWS), F32),...]
where the time goes in v2:
time: 122 us
  Pallas kernels  120 us (98%)
  local copies, waits for them, and re-layouts  1.84 us (2%)
    pallas_call x1, Pallas kernels, on_device(): pl.pallas_call(kernel, out_shape=jax.ShapeDtypeStruct((COLS, ROWS), F32),...  120 us

profile of v2, /device:TPU:1, one launch (start us, length us, event | category | flops | bytes accessed | tf_op | source)
XLA Modules:
  0.0 121.6 jit_solution(1333533830049670889)
XLA Ops:
  0.0 119.7 %two_layers.1 = f32[320,384]{1,0:T(8,128)} custom-call(s32[4]{0:T(128)} %len_ref.1, f32[1,128]{1,0:T(1,128)} %constant.2.clone.freq_ref, f32[320,384]{1,0:T(8,128)} %bitcast.7, bf16[2,128,128]{2,1,0:T(8,128)(2,1)} %bitcast.8, bf16[2,128,128]{2,1,0:T(8,128)(2,1)} %bitcast.9, bf16[2,320,1280]{2,1,0:T(8,128)(2,1)} %win_hbm.1, bf16[2,320,1024]{2,1,0:T(8,128)(2,1)} %bitcast.6), custom_call_target="tpu_custom_call" | custom-call | tf_op jit(solution)/shard_map/two_layers/pallas_call | solution.py:547
  119.7 1.8 %copy.9 = f32[384,320]{0,1:T(8,128)} copy(f32[384,320]{0,1:T(8,128)} %bitcast.5) | data formatting | bytes 983040

commit v3 on v2

--- a/solution.py
+++ b/solution.py
@@ -23,7 +23,6 @@
 PART0 = 640
 PART1 = 640
 WIDE0 = PART0 + 128
-PACKED = 120
 COPIES = 128
 MESH = pl.DeviceIdType.MESH
 F32 = jnp.float32
@@ -38,23 +37,11 @@
     return lax.broadcasted_iota(jnp.int32, shape, axis)
 
 
-def pack(block):
-    tail = block[:, 256:384]
-    low = iota((OWN, 128), 1) < 64
-    both = jnp.where(low, tail[:OWN], pltpu.roll(tail[OWN:], 64, 1))
-    return jnp.concatenate([block[:, 0:128], block[:, 128:256], both], axis=0)
-
-
-def unpack_tail(packed):
-    both = packed[2 * CHIP :]
-    return jnp.concatenate([both, pltpu.roll(both, 64, 1)], axis=0)
-
-
 def kernel(
     len_ref, freq_ref, hid_hbm, key_hbm, val_hbm, win_hbm, wout_hbm, out_ref,
-    hid_across, hid, win, wpad, wout, val, kv, hs, c0s, c1s, c0r, c1r, s0, s1,
+    hid_across, hid, win, wpad, wout, val, kv, hs, s0, s1,
     x0relay, x0dir, x0fin, x1relay, x1dir, x1fin, y1r, y0r,
-    past_ref, length_ref, cos_ref, sin_ref, gat, ob, d1r, d2r, sg, fg, str1, out_rows,
+    past_ref, length_ref, cos_ref, sin_ref, gat, ob, d1r, d2r, sg, fg, fs, str1, out_rows, out_cols,
     load_sem, send_sem, recv_sem,
 ):
     s = lax.axis_index("sample")
@@ -83,6 +70,8 @@
     to_ahead = {"sample": place(y, ahead, core)}
     to_behind = {"sample": place(y, behind, core)}
     to_other = {"sample": place(other, x, core)}
+    to_other_ahead = {"sample": place(other, ahead, core)}
+    to_other_behind = {"sample": place(other, behind, core)}
     partner = {"tensor": ring(-1)}
 
     used = [0]
@@ -118,24 +107,25 @@
         loads[name] = pltpu.make_async_copy(src, dst, load_sem.at[index])
         loads[name].start()
 
-    load("hid", 0, hid_hbm, hid_across.at[pl.ds(0, COLS)])
-    load("win0", 1, win_hbm.at[0], win.at[0])
+    load("hid", 0, hid_hbm, hid_across.at[core])
+    load(("win", 0), 1, win_hbm.at[0], win.at[0, core])
     for layer in range(LAYERS):
         load(("key", layer), 2 + 2 * layer, key_hbm.at[layer], kv.at[layer, s, 0])
         load(("val", layer), 3 + 2 * layer, val_hbm.at[layer], val.at[layer])
-    load(("wout", 0), 6, wout_hbm.at[0], wpad.at[0, pl.ds(0, COLS)])
-    load("win1", 7, win_hbm.at[1], win.at[1])
-    load(("wout", 1), 8, wout_hbm.at[1], wpad.at[1, pl.ds(0, COLS)])
-    hid_across[COLS:] = jnp.zeros((PAD - COLS, ROWS), F32)
-    for layer in range(LAYERS):
-        wpad[layer, COLS:] = jnp.zeros((PAD - COLS, 1024), BF16)
+    load(("wout", 0), 6, wout_hbm.at[0], wpad.at[0, core])
+    load(("win", 1), 7, win_hbm.at[1], win.at[1, core])
+    load(("wout", 1), 8, wout_hbm.at[1], wpad.at[1, core])
 
     barrier = pltpu.get_barrier_semaphore()
-    near = [sibling, to_ahead, to_behind, to_other]
+    near = [sibling, to_ahead, to_behind, to_other, to_other_ahead, to_other_behind]
     near += [{"tensor": ring(step)} for step in (-1, 1, 2, -2, 3)]
     for device in near:
         pl.semaphore_signal(barrier, inc=1, device_id=device, device_id_type=MESH)
     pl.semaphore_wait(barrier, len(near))
+
+    shared = ids(5)
+    send(shared + 0, hid_hbm, hid_across.at[core], sibling)
+    send(shared + 1, win_hbm.at[0], win.at[0, core], sibling)
 
     class Gather:
         def __init__(self, buf):
@@ -190,22 +180,21 @@
 
     begin_prompt(0)
 
+    send(shared + 2, wout_hbm.at[0], wpad.at[0, core], sibling)
+    send(shared + 3, win_hbm.at[1], win.at[1, core], sibling)
+    send(shared + 4, wout_hbm.at[1], wpad.at[1, core], sibling)
+
+    def my_rows(q):
+        return pl.ds(pl.multiple_of(q * CHIP + core * OWN, 8), OWN)
+
     loads["hid"].wait()
-    hid[...] = hid_across[...].T
-    for parity in range(2):
-        pieces = [hid[CHIP * q + OWN * parity : CHIP * q + OWN * parity + OWN, :COLS] for q in range(8)]
-        hs[parity] = jnp.concatenate(pieces, axis=0).astype(BF16)
-        for q in range(8):
-            squares = jnp.sum(pieces[q] * pieces[q], axis=1, keepdims=True)
-            target = s0.at[q % 4, q // 4] if parity == 0 else c0s.at[q % 4, q // 4]
-            target[:, PART0:] = jnp.broadcast_to(squares, (OWN, 128))
-    flip = core == 1
+    arrived(shared + 0, hid_across.at[1 - core])
+    hid[...] = hid_across[...].reshape(2 * COLS, ROWS).T
+    pieces = [hid[my_rows(q), :] for q in range(8)]
+    hs[...] = jnp.concatenate(pieces, axis=0).astype(BF16)
     for q in range(8):
-        zero_rows = s0[q % 4, q // 4, :, PART0:]
-        one_rows = c0s[q % 4, q // 4, :, PART0:]
-        s0[q % 4, q // 4, :, PART0:] = jnp.where(flip, one_rows, zero_rows)
-        c0s[q % 4, q // 4, :, PART0:] = jnp.where(flip, zero_rows, one_rows)
-    loads["win0"].wait()
+        squares = jnp.sum(pieces[q] * pieces[q], axis=1, keepdims=True)
+        s0[q % 4, q // 4, :, PART0:] = jnp.broadcast_to(squares, (OWN, 128))
 
     def tables():
         row = iota((OWN, 128), 0)
@@ -233,71 +222,50 @@
         length_ref[...] = length
 
     def project(layer):
-        first = ids(14)
-        sib = hs[1 - core]
-        weights = win.at[layer]
-        part = dot(sib, weights[:, PART0:])
-        c1s[...] = part.reshape(2, 4, OWN, PART1)
-        send(first + 0, c1s.at[other], c1r.at[layer, other], sibling)
-        part = dot(sib, weights[:, :PART0])
-        for q in range(8):
-            c0s[q % 4, q // 4, :, :PART0] = part[OWN * q : OWN * q + OWN]
-        send(first + 1, c0s.at[far], c0r.at[layer, far], sibling)
-        send(first + 2, c0s.at[ahead], c0r.at[layer, ahead], sibling)
-        send(first + 3, c0s.at[behind], c0r.at[layer, behind], sibling)
-        send(first + 4, c0s.at[x], c0r.at[layer, x], sibling)
-        send(first + 5, c1s.at[y], c1r.at[layer, y], sibling)
-        mine = hs[core]
-        part = dot(mine, weights[:, PART0:])
+        first = ids(8)
+        loads[("win", layer)].wait()
+        arrived(shared + 1 + 2 * layer, win.at[layer, 1 - core])
+        rows = hs[...]
+        part = dot(rows, win[layer, :, :, PART0:].reshape(2 * COLS, PART1))
         s1[...] = part.reshape(2, 4, OWN, PART1)
-        part = dot(mine, weights[:, :PART0])
+        send(first + 0, s1.at[other], y1r.at[layer], to_other)
+        part = dot(rows, win[layer, :, :, :PART0].reshape(2 * COLS, PART0))
         for q in range(8):
             s0[q % 4, q // 4, :, :PART0] = part[OWN * q : OWN * q + OWN]
-
-        def core_sum(index, total, came):
-            arrived(index, came)
-            total[...] = total[...] + came[...]
-
-        core_sum(first + 0, s1.at[other], c1r.at[layer, other])
-        send(first + 6, s1.at[other], y1r.at[layer], to_other)
-        core_sum(first + 1, s0.at[far], c0r.at[layer, far])
-        send(first + 7, s0.at[far], x0relay.at[layer], to_ahead)
-        core_sum(first + 2, s0.at[behind], c0r.at[layer, behind])
-        send(first + 8, s0.at[behind], x0dir.at[layer], to_behind)
-        core_sum(first + 3, s0.at[ahead], c0r.at[layer, ahead])
-        core_sum(first + 4, s0.at[x], c0r.at[layer, x])
-        core_sum(first + 5, s1.at[y], c1r.at[layer, y])
+        send(first + 1, s0.at[far], x0relay.at[layer], to_ahead)
+        send(first + 2, s0.at[behind], x0dir.at[layer], to_behind)
         if layer == 0:
             gathers[0].cross()
             gathers[0].along(0)
             tables()
         loads[("wout", layer)].wait()
-        wout[...] = wpad[layer].T
-        arrived(first + 7, x0relay.at[layer])
+        arrived(shared + 2 + 2 * layer, wpad.at[layer, 1 - core])
+        wout[...] = wpad[layer].reshape(2 * COLS, 1024).T
+        arrived(first + 1, x0relay.at[layer])
         s0[ahead] = s0[ahead] + x0relay[layer]
-        send(first + 9, s0.at[ahead], x0fin.at[layer], to_ahead)
-        arrived(first + 6, y1r.at[layer])
+        send(first + 3, s0.at[ahead], x0fin.at[layer], to_ahead)
+        arrived(first + 0, y1r.at[layer])
         s1[y] = s1[y] + y1r[layer]
-        send(first + 10, s1.at[y, far], x1relay.at[layer], to_ahead)
-        send(first + 11, s1.at[y, behind], x1dir.at[layer], to_behind)
+        send(first + 4, s1.at[y, far], x1relay.at[layer], to_ahead)
+        send(first + 5, s1.at[y, behind], x1dir.at[layer], to_behind)
         if layer == 0:
             gathers[0].last(0)
             gathers[0].along(1)
-        arrived(first + 10, x1relay.at[layer])
+        arrived(first + 4, x1relay.at[layer])
         s1[y, ahead] = s1[y, ahead] + x1relay[layer]
-        send(first + 12, s1.at[y, ahead], x1fin.at[layer], to_ahead)
-        arrived(first + 8, x0dir.at[layer])
-        arrived(first + 9, x0fin.at[layer])
+        send(first + 6, s1.at[y, ahead], x1fin.at[layer], to_ahead)
+        arrived(first + 2, x0dir.at[layer])
+        arrived(first + 3, x0fin.at[layer])
         s0[x] = s0[x] + x0dir[layer] + x0fin[layer]
-        send(first + 13, s0.at[x, other], y0r.at[layer], to_other)
+        send(first + 7, s0.at[x, other], y0r.at[layer], to_other)
         if layer == 0:
             gathers[0].last(1)
             gathers[0].core_side(0)
             gathers[0].core_side(1)
-        arrived(first + 11, x1dir.at[layer])
-        arrived(first + 12, x1fin.at[layer])
+        arrived(first + 5, x1dir.at[layer])
+        arrived(first + 6, x1fin.at[layer])
         part1 = s1[y, x] + x1dir[layer] + x1fin[layer]
-        arrived(first + 13, y0r.at[layer])
+        arrived(first + 7, y0r.at[layer])
         part0 = s0[x, y] + y0r[layer]
         return part0, part1
 
@@ -374,30 +342,34 @@
         for half in range(2):
             rows = attention[:, 128 * half : 128 * half + 128].T
             halves.append(jnp.concatenate([rows[OWN * h : OWN * h + OWN] for h in range(4)], axis=1))
-        gat[layer, s] = jnp.concatenate(halves, axis=0).astype(BF16)
+        gat[layer, chip] = jnp.concatenate(halves, axis=0).astype(BF16)
 
     def collect(layer):
-        gather = Gather(gat.at[layer])
-        gather.begin()
-        gather.along(0)
-        gather.cross()
-        gather.last(0)
-        gather.along(1)
+        at = ids(7)
+        buf = gat.at[layer]
+        mine = buf.at[chip]
+        send(at + 0, mine, mine, to_ahead)
+        send(at + 1, mine, mine, to_behind)
+        send(at + 3, mine, mine, to_other_ahead)
+        send(at + 4, mine, mine, to_other_behind)
+        send(at + 2, mine, mine, to_other)
+
+        def came(number, py, px):
+            block = buf.at[py * 4 + px]
+            arrived(at + number, block)
+            return block
+
+        block = came(0, y, behind)
+        send(at + 5, block, block, to_ahead)
+        block = came(3, other, behind)
+        send(at + 6, block, block, to_ahead)
 
         def product(half):
-            rows = gat[layer, pl.ds(half * 8, 8)].reshape(8 * CHIP, 512)
-            upper = dot(rows, wout[:512])
-            lower = dot(rows, wout[512:])
+            blocks = gat[layer, pl.ds(half * 4, 4)].astype(F32)
+            rows = [jnp.concatenate([blocks[q, :OWN], blocks[q, OWN:]], axis=1) for q in range(4)]
+            result = dot(jnp.concatenate(rows, axis=0).astype(BF16), wout[...])
             for q in range(4):
-                at = 2 * CHIP * q
-                block = jnp.concatenate(
-                    [
-                        upper[at : at + OWN] + lower[at + OWN : at + CHIP],
-                        upper[at + CHIP : at + CHIP + OWN] + lower[at + CHIP + OWN : at + 2 * CHIP],
-                    ],
-                    axis=0,
-                )
-                ob[half * 4 + q] = pack(block)
+                ob[half * 4 + q] = result[OWN * q : OWN * q + OWN]
 
         first = ids(7)
         early = (y + z + 1) % 2
@@ -405,12 +377,14 @@
         def hand_over(k):
             send(first + k, ob.at[chip_of(ring(-1 - k))], d1r.at[layer, k], partner)
 
-        gather.core_side(0)
+        came(1, y, ahead)
+        came(5, y, far)
         product(y)
         hand_over(early + 2)
         hand_over(early)
-        gather.last(1)
-        gather.core_side(1)
+        came(2, other, x)
+        came(4, other, ahead)
+        came(6, other, far)
         product(other)
         hand_over(3 - early)
         hand_over(1 - early)
@@ -432,69 +406,76 @@
             total = total + d2r[layer, k - 1]
         return total
 
-    def tensor_gather(buf):
+    def tensor_gather(buf, held=lambda at: None):
         first = ids(7)
         mine = buf.at[z]
         send(first + 2, mine, mine, {"tensor": ring(3)})
         send(first + 1, mine, mine, {"tensor": ring(-2)})
         send(first + 0, mine, mine, {"tensor": ring(1)})
         send(first + 3, mine, mine, partner)
+        held(z)
         for k in (1, 2, 3):
             block = buf.at[ring(k)]
             arrived(first + k - 1, block)
             send(first + 3 + k, block, block, partner)
+            held(ring(k))
         for k in (0, 1, 2, 3):
             arrived(first + 3 + k, buf.at[ring(-1 - k)])
+            held(ring(-1 - k))
 
     part0, part1 = project(0)
     attend(0, part0, part1)
-    stream = pack(hid[pl.ds(pl.multiple_of(chip_of(z) * CHIP, 8), CHIP), :]) + collect(0)
+    stream = hid[my_rows(chip_of(z)), :] + collect(0)
     str1[...] = stream
-    tail = unpack_tail(stream)
-    lane = iota((CHIP, 128), 1)
-    middle0 = stream[:CHIP]
-    middle1 = stream[CHIP : 2 * CHIP]
-    kept = jnp.where(lane < 64, tail, 0.0)
-    squares = jnp.sum(middle0 * middle0 + middle1 * middle1 + kept * kept, axis=1, keepdims=True)
+    squares = jnp.sum(stream * stream, axis=1, keepdims=True)
     square1 = squares.astype(BF16).astype(F32)
     square2 = (squares - square1).astype(BF16).astype(F32)
     square3 = squares - square1 - square2
-    kept = jnp.where(lane == 64, square1, kept)
-    kept = jnp.where(lane == 65, square2, kept)
-    kept = jnp.where(lane == 66, square3, kept)
-    sg[z] = jnp.concatenate([middle0, middle1, kept], axis=1).astype(BF16)
+    diagonal = iota((OWN, 128), 0) == iota((OWN, 128), 1)
+    line = iota((8, 128), 0)
+    extra = jnp.zeros((8, 128), F32)
+    for i, term in enumerate((square1, square2, square3)):
+        across = jnp.sum(jnp.where(diagonal, term, 0.0), axis=0, keepdims=True)
+        extra = jnp.where(line == i, across, extra)
+    tiles = [stream[:, 128 * t : 128 * t + 128] for t in range(5)]
+    sg[z] = jnp.concatenate(tiles + [extra], axis=0).astype(BF16)
     tensor_gather(sg)
     gathers[1].last(0)
     gathers[1].along(1)
     drain()
 
-    flip = core == 1
-    by_parity = [[], []]
+    pieces = []
     for q in range(8):
         block = sg[2 * (q % 4) + q // 4].astype(F32)
-        sums = jnp.sum(jnp.where(lane >= 64, block[:, 256:], 0.0), axis=1, keepdims=True)
-        sums = jnp.broadcast_to(sums, (CHIP, 128))
-        s0[q % 4, q // 4, :, PART0:] = jnp.where(flip, sums[OWN:], sums[:OWN])
-        c0s[q % 4, q // 4, :, PART0:] = jnp.where(flip, sums[:OWN], sums[OWN:])
-        for parity in range(2):
-            by_parity[parity].append(block[OWN * parity : OWN * parity + OWN, :COLS])
-    for parity in range(2):
-        hs[parity] = jnp.concatenate(by_parity[parity], axis=0).astype(BF16)
-    loads["win1"].wait()
+        across = jnp.sum(block[5 * OWN :], axis=0, keepdims=True)
+        squares = jnp.sum(jnp.where(diagonal, across, 0.0), axis=1, keepdims=True)
+        s0[q % 4, q // 4, :, PART0:] = jnp.broadcast_to(squares, (OWN, 128))
+        pieces.append(jnp.concatenate([block[OWN * t : OWN * t + OWN] for t in range(5)], axis=1))
+    hs[...] = jnp.concatenate(pieces, axis=0).astype(BF16)
     part0, part1 = project(1)
     gathers[1].last(1)
     gathers[1].core_side(0)
     gathers[1].core_side(1)
     attend(1, part0, part1)
-    fg[z] = str1[...] + collect(1)
-    tensor_gather(fg)
-    for d in range(8):
-        block = fg[d]
-        rows = pl.ds(CHIP * chip_of(d), CHIP)
-        out_rows[rows, 0:128] = block[:CHIP]
-        out_rows[rows, 128:256] = block[CHIP : 2 * CHIP]
-        out_rows[rows, 256:384] = unpack_tail(block)
-    out_ref[...] = out_rows[...].T[:COLS]
+    stream = str1[...] + collect(1)
+    for t in range(5):
+        fg[z, t] = stream[:, 128 * t : 128 * t + 128]
+    crossing = ids(8)
+
+    def hand_across(at):
+        send(crossing + at, fg.at[at, pl.ds(2 - 2 * core, 3)], fs.at[at], sibling)
+
+    tensor_gather(fg, hand_across)
+    for at in range(8):
+        for t in range(3):
+            out_rows[my_rows(chip_of(at)), 128 * t : 128 * t + 128] = fg[at, 2 * core + t]
+    for at in range(8):
+        arrived(crossing + at, fs.at[at])
+        theirs = pl.ds(pl.multiple_of(chip_of(at) * CHIP + (1 - core) * OWN, 8), OWN)
+        for t in range(3):
+            out_rows[theirs, 128 * t : 128 * t + 128] = fs[at, t]
+    out_cols[...] = out_rows[...].T
+    out_ref[...] = out_cols[pl.ds(pl.multiple_of(core * 64, 8), COLS), :]
     drain()
 
 
@@ -505,18 +486,14 @@
     freq = jnp.asarray(np.concatenate([half, half])[None, :], F32)
     vmem = pltpu.VMEM
     scratch = [
-        vmem((PAD, ROWS), F32),
-        vmem((ROWS, PAD), F32),
-        vmem((LAYERS, COLS, 1280), BF16),
-        vmem((LAYERS, PAD, 1024), BF16),
-        vmem((1024, PAD), BF16),
+        vmem((2, COLS, ROWS), F32),
+        vmem((ROWS, 2 * COLS), F32),
+        vmem((LAYERS, 2, COLS, 1280), BF16),
+        vmem((LAYERS, 2, COLS, 1024), BF16),
+        vmem((1024, 2 * COLS), BF16),
         vmem((LAYERS, 128, HEAD), BF16),
         vmem((LAYERS, 17, 2, 128, HEAD), BF16),
-        vmem((2, 192, COLS), BF16),
-        vmem((4, 2, OWN, WIDE0), F32),
-        vmem((2, 4, OWN, PART1), F32),
-        vmem((LAYERS, 4, 2, OWN, WIDE0), F32),
-        vmem((LAYERS, 2, 4, OWN, PART1), F32),
+        vmem((8 * OWN, 2 * COLS), BF16),
         vmem((4, 2, OWN, WIDE0), F32),
         vmem((2, 4, OWN, PART1), F32),
         vmem((LAYERS, 2, OWN, WIDE0), F32),
@@ -531,14 +508,16 @@
         vmem((128, 128), jnp.int32),
         vmem((OWN, 128), F32),
         vmem((OWN, 128), F32),
-        vmem((LAYERS, 16, CHIP, 512), BF16),
-        vmem((8, PACKED, 128), F32),
-        vmem((LAYERS, 4, PACKED, 128), F32),
-        vmem((LAYERS, 3, PACKED, 128), F32),
-        vmem((8, CHIP, PAD), BF16),
-        vmem((8, PACKED, 128), F32),
-        vmem((PACKED, 128), F32),
+        vmem((LAYERS, 8, CHIP, 512), BF16),
+        vmem((8, OWN, 2 * COLS), F32),
+        vmem((LAYERS, 4, OWN, 2 * COLS), F32),
+        vmem((LAYERS, 3, OWN, 2 * COLS), F32),
+        vmem((8, 128, 128), BF16),
+        vmem((8, 5, OWN, 128), F32),
+        vmem((8, 3, OWN, 128), F32),
+        vmem((OWN, 2 * COLS), F32),
         vmem((ROWS, PAD), F32),
+        vmem((PAD, ROWS), F32),
         pltpu.SemaphoreType.DMA((9,)),
         pltpu.SemaphoreType.DMA((COPIES,)),
         pltpu.SemaphoreType.DMA((COPIES,)),

time: 122 us -> 119 us (0.975)
  Pallas kernels: 120 us -> 117 us
    pallas_call x1, Pallas kernels: 120 us -> 117 us  [on_device(): pl.pallas_call(kernel, out_shape=jax.ShapeDtypeStruct((COLS, ROWS), F32),...]
where the time goes in v3:
time: 119 us
  Pallas kernels  117 us (98%)
  local copies, waits for them, and re-layouts  1.84 us (2%)
    pallas_call x1, Pallas kernels, on_device(): pl.pallas_call(kernel, out_shape=jax.ShapeDtypeStruct((COLS, ROWS), F32),...  117 us

profile of v3, /device:TPU:1, one launch (start us, length us, event | category | flops | bytes accessed | tf_op | source)
XLA Modules:
  0.0 118.9 jit_solution(15257405721568066388)
XLA Ops:
  0.0 117.0 %two_layers.1 = f32[320,384]{1,0:T(8,128)} custom-call(s32[4]{0:T(128)} %len_ref.1, f32[1,128]{1,0:T(1,128)} %constant.2.clone.freq_ref, f32[320,384]{1,0:T(8,128)} %bitcast.7, bf16[2,128,128]{2,1,0:T(8,128)(2,1)} %bitcast.8, bf16[2,128,128]{2,1,0:T(8,128)(2,1)} %bitcast.9, bf16[2,320,1280]{2,1,0:T(8,128)(2,1)} %win_hbm.1, bf16[2,320,1024]{2,1,0:T(8,128)(2,1)} %bitcast.6), custom_call_target="tpu_custom_call" | custom-call | tf_op jit(solution)/shard_map/two_layers/pallas_call | solution.py:526
  117.0 1.8 %copy.9 = f32[384,320]{0,1:T(8,128)} copy(f32[384,320]{0,1:T(8,128)} %bitcast.5) | data formatting | bytes 983040

commit v4 on v3

v4 whole, which is shorter than its diff:
```python
import jax
import jax.numpy as jnp
import numpy as np
from jax import lax
from jax.experimental import pallas as pl
from jax.experimental.pallas import tpu as pltpu
from jax.sharding import PartitionSpec as P

STEPS = 6
NPR = 4
HEADS = 8
HEAD = 128
LAYERS = 2
ROPE_BASE = 1000000.0
EPSILON = 1e-06
NEGATIVE = -1e30
WIDTH = 5120
ROWS = 384
OWN = 24
CHIP = 48
COLS = 320
PAD = 384
PART0 = 640
PART1 = 640
WIDE0 = PART0 + 128
COPIES = 176
GROUPS = (16, 8)
MESH = pl.DeviceIdType.MESH
F32 = jnp.float32
BF16 = jnp.bfloat16


def dot(a, b):
    return jnp.dot(a, b, preferred_element_type=F32)


def iota(shape, axis):
    return lax.broadcasted_iota(jnp.int32, shape, axis)


def kernel(
    len_ref, freq_ref, hid_hbm, key_hbm, val_hbm, win_hbm, wout_hbm, out_ref,
    hid_across, hid, win, wpad, wout, val, kv, cos_ref, sin_ref, past_ref, length_ref, newest, out_rows, out_cols,
    *grouped,
):
    load_sem, send_sem, recv_sem = grouped[-3:]
    s = lax.axis_index("sample")
    z = lax.axis_index("tensor")
    core = s % 2
    chip = s // 2
    x = chip % 4
    y = chip // 4
    other = 1 - y
    sigma = 1 - 2 * core
    ahead = (x + sigma + 4) % 4
    behind = (x - sigma + 4) % 4
    far = (x + 2) % 4
    delta = 2 * ((z + core) % 2) - 1

    def place(py, px, pc):
        return (py * 4 + px) * 2 + pc

    def ring(step):
        return (z + delta * step + 8) % 8

    def chip_of(at):
        return (at % 2) * 4 + at // 2

    sibling = {"sample": place(y, x, 1 - core)}
    to_ahead = {"sample": place(y, ahead, core)}
    to_behind = {"sample": place(y, behind, core)}
    to_other = {"sample": place(other, x, core)}
    to_other_ahead = {"sample": place(other, ahead, core)}
    to_other_behind = {"sample": place(other, behind, core)}
    partner = {"tensor": ring(-1)}

    used = [0]
    pending = [[], [], []]

    def ids(count):
        first = used[0]
        used[0] += count
        return first

    def send(index, src, dst, device, chain=2):
        copy = pltpu.make_async_remote_copy(
            src_ref=src, dst_ref=dst, send_sem=send_sem.at[index], recv_sem=recv_sem.at[index],
            device_id=device, device_id_type=MESH,
        )
        copy.start()
        pending[chain].append(copy)

    def arrived(index, ref):
        pltpu.make_async_remote_copy(
            src_ref=ref, dst_ref=ref, send_sem=send_sem.at[index], recv_sem=recv_sem.at[index],
            device_id=sibling, device_id_type=MESH,
        ).wait_recv()

    def drain(chain):
        for copy in pending[chain]:
            copy.wait_send()
        pending[chain].clear()

    loads = {}

    def load(name, index, src, dst):
        loads[name] = pltpu.make_async_copy(src, dst, load_sem.at[index])
        loads[name].start()

    load("hid", 0, hid_hbm, hid_across.at[core])
    load(("win", 0), 1, win_hbm.at[0], win.at[0, core])
    for layer in range(LAYERS):
        load(("key", layer), 2 + 2 * layer, key_hbm.at[layer], kv.at[layer, s, 0])
        load(("val", layer), 3 + 2 * layer, val_hbm.at[layer], val.at[layer])
    load(("wout", 0), 6, wout_hbm.at[0], wpad.at[0, core])
    load(("win", 1), 7, win_hbm.at[1], win.at[1, core])
    load(("wout", 1), 8, wout_hbm.at[1], wpad.at[1, core])

    barrier = pltpu.get_barrier_semaphore()
    near = [sibling, to_ahead, to_behind, to_other, to_other_ahead, to_other_behind]
    near += [{"tensor": ring(step)} for step in (-1, 1, 2, -2, 3)]
    for device in near:
        pl.semaphore_signal(barrier, inc=1, device_id=device, device_id_type=MESH)
    pl.semaphore_wait(barrier, len(near))

    shared = ids(5)
    send(shared + 0, hid_hbm, hid_across.at[core], sibling)
    send(shared + 1, win_hbm.at[0], win.at[0, core], sibling)

    class Gather:
        def __init__(self, buf):
            self.buf = buf
            self.first = ids(15)

        def put(self, number, py, px, device, pc=None):
            block = self.buf.at[place(py, px, core)]
            send(self.first + number, block, block, device)

        def get(self, number, py, px, pc=None):
            where = place(py, px, core if pc is None else pc)
            arrived(self.first + number, self.buf.at[where])

        def begin(self):
            self.put(0, y, x, to_other)
            self.put(1, y, x, to_ahead)
            self.put(2, y, x, to_behind)
            self.put(7, y, x, sibling)

        def cross(self):
            self.get(0, other, x)
            self.put(4, other, x, to_ahead)
            self.put(5, other, x, to_behind)
            self.put(11, other, x, sibling)

        def along(self, half):
            py, at, near_core = (y, 1, 8) if half == 0 else (other, 4, 12)
            self.get(at, py, behind)
            self.put(at + 2, py, behind, to_ahead)
            self.put(near_core, py, behind, sibling)
            self.get(at + 1, py, ahead)
            self.put(near_core + 1, py, ahead, sibling)

        def last(self, half):
            py, at, near_core = (y, 3, 10) if half == 0 else (other, 6, 14)
            self.get(at, py, far)
            self.put(near_core, py, far, sibling)

        def core_side(self, half):
            py, at = (y, 7) if half == 0 else (other, 11)
            for number, px in enumerate((x, ahead, behind, far)):
                self.get(at + number, py, px, 1 - core)

    gathers = [Gather(kv.at[layer]) for layer in range(LAYERS)]

    def begin_prompt(layer):
        loads[("key", layer)].wait()
        loads[("val", layer)].wait()
        kv[layer, s, 1] = val[layer].astype(F32).T.astype(BF16)
        gathers[layer].begin()

    begin_prompt(0)

    send(shared + 2, wout_hbm.at[0], wpad.at[0, core], sibling)
    send(shared + 3, win_hbm.at[1], win.at[1, core], sibling)
    send(shared + 4, wout_hbm.at[1], wpad.at[1, core], sibling)

    def my_rows(q):
        return pl.ds(pl.multiple_of(q * CHIP + core * OWN, 8), OWN)

    loads["hid"].wait()
    arrived(shared + 0, hid_across.at[1 - core])
    hid[...] = hid_across[...].reshape(2 * COLS, ROWS).T
    buffers = [grouped[len(NAMES) * g : len(NAMES) * g + len(NAMES)] for g in range(2)]
    buffers = [dict(zip(NAMES, refs)) for refs in buffers]
    for q in range(8):
        piece = hid[my_rows(q), :]
        buffers[0]["rows"][q] = jnp.concatenate([piece[6 * j : 6 * j + 4] for j in range(NPR)], axis=0)
        buffers[1]["rows"][q] = jnp.concatenate([piece[6 * j + 4 : 6 * j + 6] for j in range(NPR)], axis=0)

    def sample_and_step(row, g):
        sample = lax.shift_right_logical(row, 2 - g)
        return sample, row - sample * (4 - 2 * g) + 4 * g

    def tables(g):
        count = GROUPS[g]
        lane = iota((count, 128), 1)
        sample, step = sample_and_step(iota((count, 128), 0), g)
        length = jnp.zeros((count, 128), jnp.int32)
        for k in range(NPR):
            length = jnp.where(sample == k, len_ref[k], length)
        angle = (length + step).astype(F32) * freq_ref[...]
        cos_ref[g, :count] = jnp.cos(angle)
        sin_ref[g, :count] = jnp.where(lane < 64, -jnp.sin(angle), jnp.sin(angle))
        key = iota((128, 128), 0)
        query = iota((128, 128), 1)
        sample, _ = sample_and_step(query % count, g)
        length = jnp.zeros((128, 128), jnp.int32)
        start = jnp.zeros((128, 128), jnp.int32)
        offset = jnp.int32(0)
        for k in range(NPR):
            length = jnp.where(sample == k, len_ref[k], length)
            start = jnp.where(sample == k, offset, start)
            offset = offset + len_ref[k]
        past_ref[g] = key - start
        length_ref[g] = length

    def recent(g):
        key = iota((128, 128), 0)
        sample, step = sample_and_step(iota((128, 128), 1) % GROUPS[g], g)
        early_sample, early_step = sample_and_step(key, 0)
        late_sample, late_step = sample_and_step(key - 16, 1)
        seen = (key < 16) & (early_sample == sample) & (early_step <= step)
        return seen | ((key >= 16) & (key < 24) & (late_sample == sample) & (late_step <= step))

    def attend(layer, g, part0, part1):
        count = GROUPS[g]
        inverse = lax.rsqrt(part0[:, PART0:] / WIDTH + EPSILON)
        cosine = cos_ref[g, :count]
        sine = sin_ref[g, :count]

        def rotate(vector):
            return vector * cosine + pltpu.roll(vector, 64, 1) * sine

        blocks = [part0[:, HEAD * h : HEAD * h + HEAD] * inverse for h in range(5)]
        blocks += [part1[:, HEAD * h : HEAD * h + HEAD] * inverse for h in range(5)]
        queries = [rotate(block) * HEAD**-0.5 for block in blocks[:HEADS]]
        if g == 1:
            queries.append(jnp.zeros((64, HEAD), F32))
        queries = jnp.concatenate(queries, axis=0).T
        first = queries.astype(BF16)
        rest = queries - first.astype(F32)
        second = rest.astype(BF16)
        third = (rest - second.astype(F32)).astype(BF16)
        upper = jnp.concatenate([first, second], axis=0)
        if g == 0:
            newest[...] = blocks[9]
            empty = jnp.zeros((112, HEAD), F32)
            kv[layer, 16, 0] = jnp.concatenate([rotate(blocks[8]), empty], axis=0).astype(BF16)
            kv[layer, 16, 1] = jnp.concatenate([blocks[9], empty], axis=0).T.astype(BF16)
        else:
            empty = jnp.zeros((8, HEAD), F32)
            kv[layer, 16, 0, 16:32] = jnp.concatenate([rotate(blocks[8]), empty], axis=0).astype(BF16)
            empty = jnp.zeros((104, HEAD), F32)
            kv[layer, 16, 1] = jnp.concatenate([newest[...], blocks[9], empty], axis=0).T.astype(BF16)

        def visit(block, count, seen, running):
            peak, total, summed = running
            keys = kv[layer, pl.ds(block, count), 0].reshape(count * 128, HEAD)
            scores = dot(keys, third) + dot(jnp.concatenate([keys, keys], axis=1), upper)
            parts = []
            for i in range(count):
                part = scores[128 * i : 128 * i + 128] + jnp.where(seen(i), 0.0, NEGATIVE)
                maxima = jnp.max(part, axis=0, keepdims=True)
                weights = jnp.exp(part - maxima)
                sums = jnp.sum(weights, axis=0, keepdims=True)
                parts.append((maxima, sums, dot(kv[layer, block + i, 1], weights.astype(BF16))))
            higher = peak
            for maxima, _, _ in parts:
                higher = jnp.maximum(higher, maxima)
            left = jnp.exp(peak - higher)
            total = total * left
            summed = summed * left
            for maxima, sums, values in parts:
                right = jnp.exp(maxima - higher)
                total = total + sums * right
                summed = summed + values * right
            return higher, total, summed

        running = (jnp.full((1, 128), NEGATIVE, F32), jnp.zeros((1, 128), F32), jnp.zeros((HEAD, 128), F32))
        running = visit(16, 1, lambda i: recent(g), running)

        def prompt_blocks(group, running):
            def seen(i):
                past = past_ref[g] + (group * 4 + i) * 128
                return (past >= 0) & (past < length_ref[g])

            return visit(group * 4, 4, seen, running)

        _, total, summed = lax.fori_loop(0, 4, prompt_blocks, running)
        rows = (summed / total).T
        heads = [rows[count * h : count * h + count] for h in range(HEADS)]
        if g == 0:
            return jnp.concatenate(heads, axis=1).astype(BF16)
        halves = [jnp.concatenate(heads[:4], axis=1), jnp.concatenate(heads[4:], axis=1)]
        return jnp.concatenate(halves, axis=0).astype(BF16)

    def tensor_gather(buf, chain, held=lambda at: None):
        first = ids(7)
        mine = buf.at[z]
        send(first + 2, mine, mine, {"tensor": ring(3)}, chain)
        send(first + 1, mine, mine, {"tensor": ring(-2)}, chain)
        send(first + 0, mine, mine, {"tensor": ring(1)}, chain)
        send(first + 3, mine, mine, partner, chain)
        held(z)
        yield
        for k in (1, 2, 3):
            block = buf.at[ring(k)]
            arrived(first + k - 1, block)
            send(first + 3 + k, block, block, partner, chain)
            held(ring(k))
        yield
        for k in (0, 1, 2, 3):
            arrived(first + 3 + k, buf.at[ring(-1 - k)])
            held(ring(-1 - k))

    def chain(g):
        count = GROUPS[g]
        refs = buffers[g]
        s0, s1, own = refs["s0"], refs["s1"], refs["rows"]
        gat, ob = refs["gat"], refs["ob"]
        diagonal = iota((count, 128), 0) == iota((count, 128), 1)

        def put(index, src, dst, device):
            send(index, src, dst, device, g)

        for layer in range(LAYERS):
            pieces = []
            for q in range(8):
                if layer == 0:
                    piece = own[q]
                    squares = jnp.sum(piece * piece, axis=1, keepdims=True)
                else:
                    block = refs["sg"][2 * (q % 4) + q // 4].astype(F32)
                    across = jnp.sum(block[5 * count :], axis=0, keepdims=True)
                    squares = jnp.sum(jnp.where(diagonal, across, 0.0), axis=1, keepdims=True)
                    piece = jnp.concatenate([block[count * t : count * t + count] for t in range(5)], axis=1)
                s0[q % 4, q // 4, :, PART0:] = jnp.broadcast_to(squares, (count, 128))
                pieces.append(piece)
            rows = jnp.concatenate(pieces, axis=0).astype(BF16)

            first = ids(8)
            if g == 0:
                loads[("win", layer)].wait()
                arrived(shared + 1 + 2 * layer, win.at[layer, 1 - core])
            x0relay, x0dir, x0fin = (refs[name].at[layer] for name in ("x0relay", "x0dir", "x0fin"))
            x1relay, x1dir, x1fin = (refs[name].at[layer] for name in ("x1relay", "x1dir", "x1fin"))
            y1r, y0r = refs["y1r"].at[layer], refs["y0r"].at[layer]
            part = dot(rows, win[layer, :, :, PART0:].reshape(2 * COLS, PART1))
            s1[...] = part.reshape(2, 4, count, PART1)
            put(first + 0, s1.at[other], y1r, to_other)
            part = dot(rows, win[layer, :, :, :PART0].reshape(2 * COLS, PART0))
            for q in range(8):
                s0[q % 4, q // 4, :, :PART0] = part[count * q : count * q + count]
            put(first + 1, s0.at[far], x0relay, to_ahead)
            put(first + 2, s0.at[behind], x0dir, to_behind)
            yield
            if g == 0:
                if layer == 0:
                    gathers[0].cross()
                    gathers[0].along(0)
                    tables(0)
                    tables(1)
                loads[("wout", layer)].wait()
                arrived(shared + 2 + 2 * layer, wpad.at[layer, 1 - core])
                wout[layer] = wpad[layer].reshape(2 * COLS, 1024).T
            arrived(first + 1, x0relay)
            s0[ahead] = s0[ahead] + x0relay[...]
            put(first + 3, s0.at[ahead], x0fin, to_ahead)
            arrived(first + 0, y1r)
            s1[y] = s1[y] + y1r[...]
            put(first + 4, s1.at[y, far], x1relay, to_ahead)
            put(first + 5, s1.at[y, behind], x1dir, to_behind)
            yield
            if layer == 0 and g == 0:
                gathers[0].last(0)
                gathers[0].along(1)
            arrived(first + 4, x1relay)
            s1[y, ahead] = s1[y, ahead] + x1relay[...]
            put(first + 6, s1.at[y, ahead], x1fin, to_ahead)
            arrived(first + 2, x0dir)
            arrived(first + 3, x0fin)
            s0[x] = s0[x] + x0dir[...] + x0fin[...]
            put(first + 7, s0.at[x, other], y0r, to_other)
            yield
            if g == 0:
                gathers[layer].last(1)
                gathers[layer].core_side(0)
                gathers[layer].core_side(1)
            arrived(first + 5, x1dir)
            arrived(first + 6, x1fin)
            part1 = s1[y, x] + x1dir[...] + x1fin[...]
            arrived(first + 7, y0r)
            part0 = s0[x, y] + y0r[...]
            gat[layer, chip] = attend(layer, g, part0, part1)

            first = ids(7)
            mine = gat.at[layer, chip]
            put(first + 0, mine, mine, to_ahead)
            put(first + 1, mine, mine, to_behind)
            put(first + 3, mine, mine, to_other_ahead)
            put(first + 4, mine, mine, to_other_behind)
            put(first + 2, mine, mine, to_other)
            yield
            places = ((0, y, behind), (3, other, behind), (1, y, ahead), (2, other, x), (4, other, ahead))
            places += ((5, y, far), (6, other, far))
            for number, py, px in places[:2]:
                block = gat.at[layer, py * 4 + px]
                arrived(first + number, block)
                put(first + (5 if number == 0 else 6), block, block, to_ahead)
            yield
            for number, py, px in places[2:]:
                arrived(first + number, gat.at[layer, py * 4 + px])
            if g == 0:
                rows = gat[layer].reshape(8 * count, 1024)
            else:
                blocks = gat[layer].astype(F32)
                rows = [jnp.concatenate([blocks[q, :count], blocks[q, count:]], axis=1) for q in range(8)]
                rows = jnp.concatenate(rows, axis=0).astype(BF16)
            ob[...] = dot(rows, wout[layer]).reshape(8, count, 2 * COLS)

            first = ids(7)
            d1r, d2r = refs["d1r"], refs["d2r"]
            for k in (3, 2, 1, 0):
                put(first + k, ob.at[chip_of(ring(-1 - k))], d1r.at[layer, k], partner)
            if layer == 0 and g == 1:
                begin_prompt(1)
            yield
            for k in (3, 2, 1):
                at = ring(k)
                block = ob.at[chip_of(at)]
                arrived(first + k, d1r.at[layer, k])
                block[...] = block[...] + d1r[layer, k]
                put(first + 3 + k, block, d2r.at[layer, k - 1], {"tensor": at})
            arrived(first + 0, d1r.at[layer, 0])
            stream = own[chip_of(z)] + ob[chip_of(z)] + d1r[layer, 0]
            if layer == 0 and g == 1:
                gathers[1].cross()
                gathers[1].along(0)
            yield
            for k in (1, 2, 3):
                arrived(first + 3 + k, d2r.at[layer, k - 1])
                stream = stream + d2r[layer, k - 1]
            tiles = [stream[:, 128 * t : 128 * t + 128] for t in range(5)]
            if layer == 0:
                own[chip_of(z)] = stream
                squares = jnp.sum(stream * stream, axis=1, keepdims=True)
                square1 = squares.astype(BF16).astype(F32)
                square2 = (squares - square1).astype(BF16).astype(F32)
                square3 = squares - square1 - square2
                line = iota((count, 128), 0)
                extra = jnp.zeros((count, 128), F32)
                for i, term in enumerate((square1, square2, square3)):
                    across = jnp.sum(jnp.where(diagonal, term, 0.0), axis=0, keepdims=True)
                    extra = jnp.where(line == i, across, extra)
                refs["sg"][z] = jnp.concatenate(tiles + [extra], axis=0).astype(BF16)
                yield from tensor_gather(refs["sg"], g)
                if g == 1:
                    gathers[1].last(0)
                    gathers[1].along(1)
                drain(g)
            else:
                fg, fs = refs["fg"], refs["fs"]
                for t in range(5):
                    fg[z, t] = tiles[t]
                crossing = ids(8)
                refs["crossing"] = crossing

                def hand_across(at):
                    put(crossing + at, fg.at[at, pl.ds(2 - 2 * core, 3)], fs.at[at], sibling)

                yield from tensor_gather(fg, g, hand_across)
                yield

    waiting = [chain(0), chain(1)]
    while waiting:
        for each in list(waiting):
            if next(each, "end") == "end":
                waiting.remove(each)

    def in_order(early, late):
        parts = []
        for j in range(NPR):
            parts += [early[4 * j : 4 * j + 4], late[2 * j : 2 * j + 2]]
        return jnp.concatenate(parts, axis=0)

    for at in range(8):
        for t in range(3):
            both = [buffers[g]["fg"][at, 2 * core + t] for g in range(2)]
            out_rows[my_rows(chip_of(at)), 128 * t : 128 * t + 128] = in_order(*both)
    for at in range(8):
        for g in range(2):
            arrived(buffers[g]["crossing"] + at, buffers[g]["fs"].at[at])
        theirs = pl.ds(pl.multiple_of(chip_of(at) * CHIP + (1 - core) * OWN, 8), OWN)
        for t in range(3):
            both = [buffers[g]["fs"][at, t] for g in range(2)]
            out_rows[theirs, 128 * t : 128 * t + 128] = in_order(*both)
    out_cols[...] = out_rows[...].T
    out_ref[...] = out_cols[pl.ds(pl.multiple_of(core * 64, 8), COLS), :]
    for each in range(3):
        drain(each)


NAMES = (
    "rows", "s0", "s1", "x0relay", "x0dir", "x0fin", "x1relay", "x1dir", "x1fin", "y1r", "y0r",
    "gat", "ob", "d1r", "d2r", "sg", "fg", "fs",
)


def group_scratch(count):
    vmem = pltpu.VMEM
    return [
        vmem((8, count, 2 * COLS), F32),
        vmem((4, 2, count, WIDE0), F32),
        vmem((2, 4, count, PART1), F32),
        *[vmem((LAYERS, 2, count, WIDE0), F32)] * 3,
        *[vmem((LAYERS, count, PART1), F32)] * 3,
        vmem((LAYERS, 4, count, PART1), F32),
        vmem((LAYERS, count, WIDE0), F32),
        vmem((LAYERS, 8, 16, 64 * count), BF16),
        vmem((8, count, 2 * COLS), F32),
        vmem((LAYERS, 4, count, 2 * COLS), F32),
        vmem((LAYERS, 3, count, 2 * COLS), F32),
        vmem((8, 6 * count, 128), BF16),
        vmem((8, 5, count, 128), F32),
        vmem((8, 3, count, 128), F32),
    ]


def on_device(hidden_in, prompt_len, cached_prompt_keys, cached_prompt_values, query_key_value_weight, w_out):
    keys = cached_prompt_keys.reshape(LAYERS, 128, HEAD)
    values = cached_prompt_values.reshape(LAYERS, 128, HEAD)
    half = np.power(ROPE_BASE, -2.0 * np.arange(64) / HEAD)
    freq = jnp.asarray(np.concatenate([half, half])[None, :], F32)
    vmem = pltpu.VMEM
    scratch = [
        vmem((2, COLS, ROWS), F32),
        vmem((ROWS, 2 * COLS), F32),
        vmem((LAYERS, 2, COLS, 1280), BF16),
        vmem((LAYERS, 2, COLS, 1024), BF16),
        vmem((LAYERS, 1024, 2 * COLS), BF16),
        vmem((LAYERS, 128, HEAD), BF16),
        vmem((LAYERS, 17, 2, 128, HEAD), BF16),
        vmem((2, 16, 128), F32),
        vmem((2, 16, 128), F32),
        vmem((2, 128, 128), jnp.int32),
        vmem((2, 128, 128), jnp.int32),
        vmem((16, HEAD), F32),
        vmem((ROWS, PAD), F32),
        vmem((PAD, ROWS), F32),
        *group_scratch(GROUPS[0]),
        *group_scratch(GROUPS[1]),
        pltpu.SemaphoreType.DMA((9,)),
        pltpu.SemaphoreType.DMA((COPIES,)),
        pltpu.SemaphoreType.DMA((COPIES,)),
    ]
    hbm = pl.BlockSpec(memory_space=pl.ANY)
    out = pl.pallas_call(
        kernel,
        out_shape=jax.ShapeDtypeStruct((COLS, ROWS), F32),
        in_specs=[
            pl.BlockSpec(memory_space=pltpu.SMEM),
            pl.BlockSpec(memory_space=pltpu.VMEM),
            hbm, hbm, hbm, hbm, hbm,
        ],
        out_specs=pl.BlockSpec(memory_space=pltpu.VMEM),
        scratch_shapes=scratch,
        compiler_params=pltpu.CompilerParams(
            collective_id=0, has_side_effects=True, vmem_limit_bytes=60 * 1024 * 1024
        ),
        name="two_layers",
    )(prompt_len, freq, hidden_in.T, keys, values, query_key_value_weight, w_out.transpose(0, 2, 1))
    return out.T


def solution(mesh):
    return jax.shard_map(
        on_device,
        mesh=mesh,
        in_specs=(
            P("prompt", "sample"),
            P("prompt"),
            P(None, ("prompt", "sample"), "tensor", None),
            P(None, ("prompt", "sample"), "tensor", None),
            P(None, "sample", "tensor"),
            P(None, "tensor", "sample"),
        ),
        out_specs=P("prompt", "sample"),
        check_vma=False,
    )
```

time: 119 us -> 107 us (0.90)
  Pallas kernels: 117 us -> 104 us
    pallas_call x1, Pallas kernels: 117 us -> 104 us  [on_device(): pl.pallas_call(kernel, out_shape=jax.ShapeDtypeStruct((COLS, ROWS), F32),...]
where the time goes in v4:
time: 107 us; the launch traced here: 106 us
  Pallas kernels  104 us (97%)
  local copies, waits for them, and re-layouts  1.84 us (2%)
    pallas_call x1, Pallas kernels, on_device(): pl.pallas_call(kernel, out_shape=jax.ShapeDtypeStruct((COLS, ROWS), F32),...  104 us

profile of v4, /device:TPU:1, one launch (start us, length us, event | category | flops | bytes accessed | tf_op | source)
XLA Modules:
  0.0 106.3 jit_solution(13853403216775332223)
XLA Ops:
  0.0 104.5 %two_layers.1 = f32[320,384]{1,0:T(8,128)} custom-call(s32[4]{0:T(128)} %len_ref.1, f32[1,128]{1,0:T(1,128)} %constant.2.clone.freq_ref, f32[320,384]{1,0:T(8,128)} %bitcast.7, bf16[2,128,128]{2,1,0:T(8,128)(2,1)} %bitcast.8, bf16[2,128,128]{2,1,0:T(8,128)(2,1)} %bitcast.9, bf16[2,320,1280]{2,1,0:T(8,128)(2,1)} %win_hbm.1, bf16[2,320,1024]{2,1,0:T(8,128)(2,1)} %bitcast.6), custom_call_target="tpu_custom_call" | custom-call | tf_op jit(solution)/shard_map/two_layers/pallas_call | solution.py:567
  104.5 1.8 %copy.9 = f32[384,320]{0,1:T(8,128)} copy(f32[384,320]{0,1:T(8,128)} %bitcast.5) | data formatting | bytes 983040

commit v5 on v4

--- a/solution.py
+++ b/solution.py
@@ -23,7 +23,7 @@
 PART0 = 640
 PART1 = 640
 WIDE0 = PART0 + 128
-COPIES = 176
+COPIES = 192
 GROUPS = (16, 8)
 MESH = pl.DeviceIdType.MESH
 F32 = jnp.float32
@@ -123,9 +123,11 @@
         pl.semaphore_signal(barrier, inc=1, device_id=device, device_id_type=MESH)
     pl.semaphore_wait(barrier, len(near))
 
-    shared = ids(5)
+    shared = ids(6)
     send(shared + 0, hid_hbm, hid_across.at[core], sibling)
-    send(shared + 1, win_hbm.at[0], win.at[0, core], sibling)
+    last_half, first_half = pl.ds(PART0, PART1), pl.ds(0, PART0)
+    send(shared + 1, win_hbm.at[0, :, last_half], win.at[0, core, :, last_half], sibling)
+    send(shared + 5, win_hbm.at[0, :, first_half], win.at[0, core, :, first_half], sibling)
 
     class Gather:
         def __init__(self, buf):
@@ -196,6 +198,16 @@
         piece = hid[my_rows(q), :]
         buffers[0]["rows"][q] = jnp.concatenate([piece[6 * j : 6 * j + 4] for j in range(NPR)], axis=0)
         buffers[1]["rows"][q] = jnp.concatenate([piece[6 * j + 4 : 6 * j + 6] for j in range(NPR)], axis=0)
+
+    gathers[0].cross()
+    gathers[0].along(0)
+
+    def turn(layer, quarter):
+        if quarter == 0:
+            loads[("wout", layer)].wait()
+            arrived(shared + 2 + 2 * layer, wpad.at[layer, 1 - core])
+        part = slice(256 * quarter, 256 * quarter + 256)
+        wout[layer, part] = wpad[layer, :, :, part].reshape(2 * COLS, 256).T
 
     def sample_and_step(row, g):
         sample = lax.shift_right_logical(row, 2 - g)
@@ -348,59 +360,83 @@
                 pieces.append(piece)
             rows = jnp.concatenate(pieces, axis=0).astype(BF16)
 
-            first = ids(8)
+            first = ids(14)
             if g == 0:
                 loads[("win", layer)].wait()
-                arrived(shared + 1 + 2 * layer, win.at[layer, 1 - core])
+                if layer == 0:
+                    arrived(shared + 1, win.at[0, 1 - core, :, last_half])
+                else:
+                    arrived(shared + 3, win.at[1, 1 - core])
             x0relay, x0dir, x0fin = (refs[name].at[layer] for name in ("x0relay", "x0dir", "x0fin"))
             x1relay, x1dir, x1fin = (refs[name].at[layer] for name in ("x1relay", "x1dir", "x1fin"))
             y1r, y0r = refs["y1r"].at[layer], refs["y0r"].at[layer]
             part = dot(rows, win[layer, :, :, PART0:].reshape(2 * COLS, PART1))
             s1[...] = part.reshape(2, 4, count, PART1)
-            put(first + 0, s1.at[other], y1r, to_other)
+            for number, px in enumerate((far, behind, ahead, x)):
+                put(first + number, s1.at[other, px], y1r.at[px], to_other)
+            if g == 0 and layer == 0:
+                arrived(shared + 5, win.at[0, 1 - core, :, first_half])
             part = dot(rows, win[layer, :, :, :PART0].reshape(2 * COLS, PART0))
             for q in range(8):
                 s0[q % 4, q // 4, :, :PART0] = part[count * q : count * q + count]
-            put(first + 1, s0.at[far], x0relay, to_ahead)
-            put(first + 2, s0.at[behind], x0dir, to_behind)
+            for number, py in enumerate((other, y)):
+                put(first + 4 + number, s0.at[far, py], x0relay.at[py], to_ahead)
+                put(first + 6 + number, s0.at[behind, py], x0dir.at[py], to_behind)
+            if g == 1 and layer == 0:
+                tables(0)
+                tables(1)
+                turn(0, 0)
+            elif g == 1:
+                turn(1, 2)
+            yield
+            if g == 0 and layer == 0:
+                gathers[0].last(0)
+                gathers[0].along(1)
+
+            def pass_on(number, py):
+                arrived(first + 4 + number, x0relay.at[py])
+                s0[ahead, py] = s0[ahead, py] + x0relay[py]
+                put(first + 8 + number, s0.at[ahead, py], x0fin.at[py], to_ahead)
+
+            pass_on(0, other)
+            for number, px, to, device in ((0, far, x1relay, to_ahead), (1, behind, x1dir, to_behind)):
+                arrived(first + number, y1r.at[px])
+                s1[y, px] = s1[y, px] + y1r[px]
+                put(first + 10 + number, s1.at[y, px], to, device)
+            pass_on(1, y)
+            if g == 1 and layer == 0:
+                turn(0, 1)
+                turn(0, 2)
+            elif g == 1:
+                turn(1, 3)
+            yield
+            if g == 0 and layer == 0:
+                gathers[0].last(1)
+            arrived(first + 6, x0dir.at[other])
+            arrived(first + 8, x0fin.at[other])
+            s0[x, other] = s0[x, other] + x0dir[other] + x0fin[other]
+            put(first + 13, s0.at[x, other], y0r, to_other)
+            arrived(first + 10, x1relay)
+            arrived(first + 2, y1r.at[ahead])
+            s1[y, ahead] = s1[y, ahead] + y1r[ahead] + x1relay[...]
+            put(first + 12, s1.at[y, ahead], x1fin, to_ahead)
+            if g == 1 and layer == 0:
+                turn(0, 3)
             yield
             if g == 0:
-                if layer == 0:
-                    gathers[0].cross()
-                    gathers[0].along(0)
-                    tables(0)
-                    tables(1)
-                loads[("wout", layer)].wait()
-                arrived(shared + 2 + 2 * layer, wpad.at[layer, 1 - core])
-                wout[layer] = wpad[layer].reshape(2 * COLS, 1024).T
-            arrived(first + 1, x0relay)
-            s0[ahead] = s0[ahead] + x0relay[...]
-            put(first + 3, s0.at[ahead], x0fin, to_ahead)
-            arrived(first + 0, y1r)
-            s1[y] = s1[y] + y1r[...]
-            put(first + 4, s1.at[y, far], x1relay, to_ahead)
-            put(first + 5, s1.at[y, behind], x1dir, to_behind)
-            yield
-            if layer == 0 and g == 0:
-                gathers[0].last(0)
-                gathers[0].along(1)
-            arrived(first + 4, x1relay)
-            s1[y, ahead] = s1[y, ahead] + x1relay[...]
-            put(first + 6, s1.at[y, ahead], x1fin, to_ahead)
-            arrived(first + 2, x0dir)
-            arrived(first + 3, x0fin)
-            s0[x] = s0[x] + x0dir[...] + x0fin[...]
-            put(first + 7, s0.at[x, other], y0r, to_other)
-            yield
-            if g == 0:
-                gathers[layer].last(1)
+                if layer == 1:
+                    gathers[1].last(1)
                 gathers[layer].core_side(0)
                 gathers[layer].core_side(1)
-            arrived(first + 5, x1dir)
-            arrived(first + 6, x1fin)
-            part1 = s1[y, x] + x1dir[...] + x1fin[...]
-            arrived(first + 7, y0r)
-            part0 = s0[x, y] + y0r[...]
+            arrived(first + 3, y1r.at[x])
+            arrived(first + 11, x1dir)
+            arrived(first + 12, x1fin)
+            part1 = s1[y, x] + y1r[x] + x1dir[...] + x1fin[...]
+            arrived(first + 7, x0dir.at[y])
+            arrived(first + 9, x0fin.at[y])
+            part0 = s0[x, y] + x0dir[y] + x0fin[y]
+            arrived(first + 13, y0r)
+            part0 = part0 + y0r[...]
             gat[layer, chip] = attend(layer, g, part0, part1)
 
             first = ids(7)
@@ -434,6 +470,7 @@
                 put(first + k, ob.at[chip_of(ring(-1 - k))], d1r.at[layer, k], partner)
             if layer == 0 and g == 1:
                 begin_prompt(1)
+                turn(1, 0)
             yield
             for k in (3, 2, 1):
                 at = ring(k)
@@ -446,6 +483,7 @@
             if layer == 0 and g == 1:
                 gathers[1].cross()
                 gathers[1].along(0)
+                turn(1, 1)
             yield
             for k in (1, 2, 3):
                 arrived(first + 3 + k, d2r.at[layer, k - 1])

time: 107 us -> 106 us (level)
  no operation moved by 1% of the time
where the time goes in v5:
time: 106 us; the launch traced here: 105 us
  Pallas kernels  103 us (97%)
  local copies, waits for them, and re-layouts  1.84 us (2%)
    pallas_call x1, Pallas kernels, on_device(): pl.pallas_call(kernel, out_shape=jax.ShapeDtypeStruct((COLS, ROWS), F32),...  103 us

profile of v5, /device:TPU:1, one launch (start us, length us, event | category | flops | bytes accessed | tf_op | source)
XLA Modules:
  0.0 105.3 jit_solution(3499063431139373222)
XLA Ops:
  0.0 103.5 %two_layers.1 = f32[320,384]{1,0:T(8,128)} custom-call(s32[4]{0:T(128)} %len_ref.1, f32[1,128]{1,0:T(1,128)} %constant.2.clone.freq_ref, f32[320,384]{1,0:T(8,128)} %bitcast.7, bf16[2,128,128]{2,1,0:T(8,128)(2,1)} %bitcast.8, bf16[2,128,128]{2,1,0:T(8,128)(2,1)} %bitcast.9, bf16[2,320,1280]{2,1,0:T(8,128)(2,1)} %win_hbm.1, bf16[2,320,1024]{2,1,0:T(8,128)(2,1)} %bitcast.6), custom_call_target="tpu_custom_call" | custom-call | tf_op jit(solution)/shard_map/two_layers/pallas_call | solution.py:605
  103.5 1.8 %copy.9 = f32[384,320]{0,1:T(8,128)} copy(f32[384,320]{0,1:T(8,128)} %bitcast.5) | data formatting | bytes 983040

commit v6 on v5

--- a/solution.py
+++ b/solution.py
@@ -182,9 +182,6 @@
 
     begin_prompt(0)
 
-    send(shared + 2, wout_hbm.at[0], wpad.at[0, core], sibling)
-    send(shared + 3, win_hbm.at[1], win.at[1, core], sibling)
-    send(shared + 4, wout_hbm.at[1], wpad.at[1, core], sibling)
 
     def my_rows(q):
         return pl.ds(pl.multiple_of(q * CHIP + core * OWN, 8), OWN)
@@ -385,9 +382,8 @@
             if g == 1 and layer == 0:
                 tables(0)
                 tables(1)
-                turn(0, 0)
             elif g == 1:
-                turn(1, 2)
+                turn(1, 0)
             yield
             if g == 0 and layer == 0:
                 gathers[0].last(0)
@@ -404,14 +400,13 @@
                 s1[y, px] = s1[y, px] + y1r[px]
                 put(first + 10 + number, s1.at[y, px], to, device)
             pass_on(1, y)
-            if g == 1 and layer == 0:
-                turn(0, 1)
-                turn(0, 2)
-            elif g == 1:
-                turn(1, 3)
+            if g == 1 and layer == 1:
+                turn(1, 1)
+                turn(1, 2)
             yield
             if g == 0 and layer == 0:
                 gathers[0].last(1)
+                send(shared + 2, wout_hbm.at[0], wpad.at[0, core], sibling)
             arrived(first + 6, x0dir.at[other])
             arrived(first + 8, x0fin.at[other])
             s0[x, other] = s0[x, other] + x0dir[other] + x0fin[other]
@@ -420,8 +415,8 @@
             arrived(first + 2, y1r.at[ahead])
             s1[y, ahead] = s1[y, ahead] + y1r[ahead] + x1relay[...]
             put(first + 12, s1.at[y, ahead], x1fin, to_ahead)
-            if g == 1 and layer == 0:
-                turn(0, 3)
+            if g == 1 and layer == 1:
+                turn(1, 3)
             yield
             if g == 0:
                 if layer == 1:
@@ -446,6 +441,10 @@
             put(first + 3, mine, mine, to_other_ahead)
             put(first + 4, mine, mine, to_other_behind)
             put(first + 2, mine, mine, to_other)
+            if g == 1 and layer == 0:
+                send(shared + 3, win_hbm.at[1], win.at[1, core], sibling)
+                turn(0, 0)
+                turn(0, 1)
             yield
             places = ((0, y, behind), (3, other, behind), (1, y, ahead), (2, other, x), (4, other, ahead))
             places += ((5, y, far), (6, other, far))
@@ -453,6 +452,9 @@
                 block = gat.at[layer, py * 4 + px]
                 arrived(first + number, block)
                 put(first + (5 if number == 0 else 6), block, block, to_ahead)
+            if g == 1 and layer == 0:
+                turn(0, 2)
+                turn(0, 3)
             yield
             for number, py, px in places[2:]:
                 arrived(first + number, gat.at[layer, py * 4 + px])
@@ -470,7 +472,6 @@
                 put(first + k, ob.at[chip_of(ring(-1 - k))], d1r.at[layer, k], partner)
             if layer == 0 and g == 1:
                 begin_prompt(1)
-                turn(1, 0)
             yield
             for k in (3, 2, 1):
                 at = ring(k)
@@ -483,7 +484,6 @@
             if layer == 0 and g == 1:
                 gathers[1].cross()
                 gathers[1].along(0)
-                turn(1, 1)
             yield
             for k in (1, 2, 3):
                 arrived(first + 3 + k, d2r.at[layer, k - 1])
@@ -505,6 +505,7 @@
                 if g == 1:
                     gathers[1].last(0)
                     gathers[1].along(1)
+                    send(shared + 4, wout_hbm.at[1], wpad.at[1, core], sibling)
                 drain(g)
             else:
                 fg, fs = refs["fg"], refs["fs"]

time: 106 us -> 106 us (level)
  no operation moved by 1% of the time
where the time goes in v6:
time: 106 us
  Pallas kernels  104 us (98%)
  local copies, waits for them, and re-layouts  1.84 us (2%)
    pallas_call x1, Pallas kernels, on_device(): pl.pallas_call(kernel, out_shape=jax.ShapeDtypeStruct((COLS, ROWS), F32),...  104 us

profile of v6, /device:TPU:1, one launch (start us, length us, event | category | flops | bytes accessed | tf_op | source)
XLA Modules:
  0.0 106.1 jit_solution(78464128243007402)
XLA Ops:
  0.0 104.2 %two_layers.1 = f32[320,384]{1,0:T(8,128)} custom-call(s32[4]{0:T(128)} %len_ref.1, f32[1,128]{1,0:T(1,128)} %constant.2.clone.freq_ref, f32[320,384]{1,0:T(8,128)} %bitcast.7, bf16[2,128,128]{2,1,0:T(8,128)(2,1)} %bitcast.8, bf16[2,128,128]{2,1,0:T(8,128)(2,1)} %bitcast.9, bf16[2,320,1280]{2,1,0:T(8,128)(2,1)} %win_hbm.1, bf16[2,320,1024]{2,1,0:T(8,128)(2,1)} %bitcast.6), custom_call_target="tpu_custom_call" | custom-call | tf_op jit(solution)/shard_map/two_layers/pallas_call | solution.py:606
  104.2 1.8 %copy.9 = f32[384,320]{0,1:T(8,128)} copy(f32[384,320]{0,1:T(8,128)} %bitcast.5) | data formatting | bytes 983040

commit v7 on v5

--- a/solution.py
+++ b/solution.py
@@ -308,7 +308,7 @@
 
             return visit(group * 4, 4, seen, running)
 
-        _, total, summed = lax.fori_loop(0, 4, prompt_blocks, running)
+        _, total, summed = lax.fori_loop(0, 4, prompt_blocks, running, unroll=4)
         rows = (summed / total).T
         heads = [rows[count * h : count * h + count] for h in range(HEADS)]
         if g == 0:

time: 106 us -> 104 us (0.981)
    pallas_call x1, Pallas kernels: 103 us -> 102 us  [on_device(): pl.pallas_call(kernel, out_shape=jax.ShapeDtypeStruct((COLS, ROWS), F32),...]
where the time goes in v7:
time: 104 us
  Pallas kernels  102 us (98%)
  local copies, waits for them, and re-layouts  1.84 us (2%)
    pallas_call x1, Pallas kernels, on_device(): pl.pallas_call(kernel, out_shape=jax.ShapeDtypeStruct((COLS, ROWS), F32),...  102 us

profile of v7, /device:TPU:1, one launch (start us, length us, event | category | flops | bytes accessed | tf_op | source)
XLA Modules:
  0.0 104.2 jit_solution(2416970602221087504)
XLA Ops:
  0.0 102.4 %two_layers.1 = f32[320,384]{1,0:T(8,128)} custom-call(s32[4]{0:T(128)} %len_ref.1, f32[1,128]{1,0:T(1,128)} %constant.2.clone.freq_ref, f32[320,384]{1,0:T(8,128)} %bitcast.7, bf16[2,128,128]{2,1,0:T(8,128)(2,1)} %bitcast.8, bf16[2,128,128]{2,1,0:T(8,128)(2,1)} %bitcast.9, bf16[2,320,1280]{2,1,0:T(8,128)(2,1)} %win_hbm.1, bf16[2,320,1024]{2,1,0:T(8,128)(2,1)} %bitcast.6), custom_call_target="tpu_custom_call" | custom-call | tf_op jit(solution)/shard_map/two_layers/pallas_call | solution.py:605
  102.4 1.8 %copy.9 = f32[384,320]{0,1:T(8,128)} copy(f32[384,320]{0,1:T(8,128)} %bitcast.5) | data formatting | bytes 983040
